TPU v7x, 32 devices: a whole 2x2x4 slice. The times are simulated.
32 devices in a mesh: sec: 16 (over z, y, core), op: 2 (over x).
Axes of the slice: x: 2, y: 2, z: 4, core: 2. Of those that a mesh axis runs over, the one named last changes fastest.
Arguments:
- wave: bfloat16 [96, 256, 256], P('sec', 'op'), may hold values from -6 to 6
- left_ops: bfloat16 [96, 16, 256, 256], P('sec', 'op'), may hold values from -0.125 to 0.125
- right_ops: bfloat16 [96, 16, 256, 256], P('sec', 'op'), may hold values from -0.375 to 0.375
- owner_map: int32 [96, 5], P('sec'), may hold values from 0 to 15, all different within a row; in each aligned block of 6 rows (0 to 5, 6 to 11, ...) at most 3 rows name the same one
- local_map: int32 [96, 5], P('sec'), may hold values from 0 to 5
- op_class: int32 [16], P('op'), may hold values from 0 to 4
Outputs:
- applied: bfloat16 [96, 256, 256], P('sec', 'op')
Inputs may be any that keep to these rules, and one draw needn't show every extreme that they name: `owner_map`: each row names 5 different owners; among the rows of one sec index no owner is named more than 3 times, and that count is reached.
All inputs are finite; a program needn't handle non-finite values.
Results may differ from a plain program's by a relative error of at most 0.0049.
Values may be sent and summed in bfloat16 or wider, within the bound.
No kernel may reach another device: no remote copies, remote signals or barrier semaphores. Data moves between devices by JAX's collectives and lax.ppermute only.
A program may use at most 128 MiB of HBM per device.

v0:
```python
import functools

import jax
import jax.numpy as jnp
from jax import lax
from jax.experimental import pallas as pl
from jax.experimental.pallas import tpu as pltpu
from jax.sharding import Mesh, PartitionSpec as P

ORDER, START, SECTOR, CLASS, LATER = range(5)
TABLE = (8, 128)
LIMITS = dict(table=4, sent=8, load=32, fill=8, product=24)


def ring_position(chip, chips):
    return jnp.where(lax.rem(chip, 2) == 0, lax.div(chip, 2), chips - 1 - lax.div(chip, 2))


def table_kernel(sizes, early, owner_map, local_map, op_class, wave, *refs):
    targets, terms, classes, op_size, chips = sizes
    half = chips // 2
    core = lax.axis_index("core")
    place = ring_position(lax.axis_index("chip"), chips)
    table_out, wave_out, table, unit_of, filled, sems = refs
    wave_copy = pltpu.make_async_copy(wave, wave_out, sems.at[0])
    wave_copy.start()

    @pl.loop(0, 2 * chips)
    def _(u):
        filled[u] = 0

    @pl.loop(0, targets)
    def _(t):
        @pl.loop(0, classes)
        def _(c):
            r = t * classes + c
            owner = owner_map[t, c]
            owner_core = owner & 1
            chip = owner >> 1
            position = jnp.where((chip & 1) == 0, chip >> 1, chips - 1 - (chip >> 1))
            offset = position - place
            offset = jnp.where(offset < 0, offset + chips, offset)
            distance = jnp.minimum(offset, chips - offset)
            end = (distance == 0) | (distance == half)
            holder = jnp.where(end, owner_core, jnp.where(offset > half, 0, 1))
            unit = jnp.where(distance == 0, 0, 2 * distance - jnp.where(owner_core == holder, 1, 0))
            away = jnp.where(holder == core, 0, 1)
            slot = unit + away * chips
            unit_of[r] = slot
            filled[slot] = filled[slot] + 1
            table[SECTOR, r] = local_map[t, c]
            table[LATER, r] = jnp.where((away == 1) & (unit >= early), 1, 0)

    for o in range(terms):
        table[CLASS, o] = op_class[o]

    def place_unit(u, at):
        table[START, u] = at
        count = filled[u]
        filled[u] = at
        return at + count

    table[START, 2 * chips] = lax.fori_loop(0, 2 * chips, place_unit, jnp.int32(0))

    @pl.loop(0, targets * classes)
    def _(r):
        u = unit_of[r]
        at = filled[u]
        table[ORDER, at] = r
        filled[u] = at + 1

    out = pltpu.make_async_copy(table, table_out, sems.at[1])
    out.start()
    out.wait()
    wave_copy.wait()


def fetch(unit, sector, target, sem):
    op_size = len(unit)
    me = lax.axis_index("op")
    for j, source in enumerate(unit):
        pltpu.make_async_copy(source.at[sector], target.at[lax.rem(me + j, op_size)], sem).start()


def read_table(source, target, sem):
    copy = pltpu.make_async_copy(source, target, sem)
    copy.start()
    copy.wait()


def grouped(refs, size):
    return [refs[i : i + size] for i in range(0, len(refs), size)]


def sent_kernel(sizes, low, high, asked_in, *refs):
    chips, op_size = sizes[4], sizes[3]
    *units, sent, table, slot_sems, sem = refs
    read_table(asked_in, table, sem)
    skipped = table[START, chips + low]
    for u, unit in enumerate(grouped(units, op_size), low):

        @pl.loop(table[START, chips + u], table[START, chips + u + 1])
        def _(i):
            slot = i - skipped
            fetch(unit, table[SECTOR, table[ORDER, i]], sent.at[slot], slot_sems.at[slot])

    @pl.loop(0, table[START, chips + high] - skipped)
    def _(slot):
        pltpu.make_async_copy(sent.at[slot], sent.at[slot], slot_sems.at[slot]).wait()


def fetch_own(units, low, table, blocks, block_sems):
    for u, unit in enumerate(units, low):

        @pl.loop(table[START, u], table[START, u + 1])
        def _(i):
            r = table[ORDER, i]
            fetch(unit, table[SECTOR, r], blocks.at[r], block_sems.at[r])


def fetch_received(received, first, last, table, blocks, block_sems):
    skipped = table[START, first]

    @pl.loop(skipped, table[START, last])
    def _(i):
        r = table[ORDER, i]
        pltpu.make_async_copy(received.at[i - skipped], blocks.at[r], block_sems.at[r]).start()


def wait_blocks(first, last, table, blocks, block_sems):
    @pl.loop(table[START, first], table[START, last])
    def _(i):
        r = table[ORDER, i]
        pltpu.make_async_copy(blocks.at[r], blocks.at[r], block_sems.at[r]).wait()


def load_kernel(sizes, early, table_in, left, right, *refs):
    *units, lefts, rights, blocks, table, block_sems, sems = refs
    loads = [
        pltpu.make_async_copy(left, lefts, sems.at[0]),
        pltpu.make_async_copy(right, rights, sems.at[1]),
    ]
    for load in loads:
        load.start()
    read_table(table_in, table, sems.at[2])
    fetch_own(grouped(units, sizes[3]), 0, table, blocks, block_sems)
    wait_blocks(0, early, table, blocks, block_sems)
    for load in loads:
        load.wait()


def fill_kernel(sizes, early, table_in, received, *refs):
    chips = sizes[4]
    *units, _, blocks, table, block_sems, sem = refs
    read_table(table_in, table, sem)
    fetch_received(received, chips, chips + early, table, blocks, block_sems)
    fetch_own(grouped(units, sizes[3]), early, table, blocks, block_sems)
    wait_blocks(early, chips + early, table, blocks, block_sems)


def product_kernel(sizes, early, first, count, table_in, received, lefts, rights, _, *refs):
    targets, terms, classes, op_size, chips = sizes
    keep, send, blocks, table, block_sems, sem = refs
    size = lefts.shape[-1]
    rows = size // op_size
    me = lax.axis_index("op")
    read_table(table_in, table, sem)
    if first == 0:
        fetch_received(received, chips + early, 2 * chips, table, blocks, block_sems)
        if count < targets:
            wait_blocks(chips + early, 2 * chips, table, blocks, block_sems)

    @pl.loop(0, count)
    def _(step):
        t = first + step

        if count == targets:

            @pl.loop(0, classes)
            def _(c):
                r = t * classes + c

                @pl.when(table[LATER, r] == 1)
                def _():
                    pltpu.make_async_copy(blocks.at[r], blocks.at[r], block_sems.at[r]).wait()

        lifted = []
        for o in range(terms):
            block = blocks[t * classes + table[CLASS, o]].reshape(size, size)
            lifted.append(
                jnp.dot(lefts[t, o], block, preferred_element_type=jnp.float32).astype(jnp.bfloat16)
            )
        total = lax.dot_general(
            jnp.concatenate(lifted, axis=1),
            jnp.concatenate([rights[t, o] for o in range(terms)], axis=1),
            (((1,), (1,)), ((), ())),
            preferred_element_type=jnp.float32,
        )
        for j in range(op_size):
            part = total[j * rows : (j + 1) * rows]
            distance = lax.rem(j + op_size - me, op_size)

            @pl.when(distance == 0)
            def _():
                keep[step] = part

            @pl.when(distance != 0)
            def _():
                send[distance - 1, step] = part.astype(jnp.bfloat16)


def held_kernel(source, out):
    del source, out


def shards(wave, left_ops, right_ops, owner_map, local_map, op_class):
    chips, op_size = lax.axis_size("chip"), lax.axis_size("op")
    targets, terms, size, _ = left_ops.shape
    sec_dev, rows, _ = wave.shape
    classes = owner_map.shape[1]
    half = chips // 2
    asked = targets * classes
    sizes = (targets, terms, classes, op_size, chips)
    early = chips - 3
    most = max(2, (asked + 2 * chips - 1) // (2 * chips) + 1)
    ring = list(range(0, chips, 2)) + list(range(1, chips, 2))[::-1]

    def hop(x):
        pairs = [
            (2 * ring[i] + core, 2 * ring[(i + 1 - 2 * core) % chips] + core)
            for i in range(chips)
            for core in range(2)
        ]
        return lax.ppermute(x, ("chip", "core"), pairs)

    def swap(x):
        return lax.ppermute(x, "core", [(0, 1), (1, 0)])

    def across(x):
        return [
            lax.ppermute(x, "op", [((q + j) % op_size, q) for q in range(op_size)])
            for j in range(1, op_size)
        ]

    whole = pl.BlockSpec(memory_space=pltpu.VMEM)
    scalars = pl.BlockSpec(memory_space=pltpu.SMEM)
    apart = pl.BlockSpec(memory_space=pl.ANY)
    def call(kernel, name, operands, outs, scratch, specs=None, aliases={}, flops=0):
        return pl.pallas_call(
            kernel,
            name=name,
            in_specs=specs or [whole] + [apart] * (len(operands) - 1),
            out_specs=[whole] * len(outs),
            out_shape=outs,
            input_output_aliases=aliases,
            scratch_shapes=[pltpu.SMEM(TABLE, jnp.int32)] + scratch,
            compiler_params=pltpu.CompilerParams(vmem_limit_bytes=LIMITS[name] * 1024 * 1024),
            cost_estimate=pl.CostEstimate(
                flops=flops, bytes_accessed=sum(2 * x.size for x in outs), transcendentals=0
            ),
        )(*operands)

    table, wave_near = call(
        functools.partial(table_kernel, sizes, early),
        "table",
        [owner_map, local_map, op_class, wave],
        [jax.ShapeDtypeStruct(TABLE, jnp.int32), jax.ShapeDtypeStruct(wave.shape, wave.dtype)],
        [
            pltpu.SMEM((asked,), jnp.int32),
            pltpu.SMEM((2 * chips,), jnp.int32),
            pltpu.SemaphoreType.DMA((2,)),
        ],
        [scalars] * 3 + [apart],
    )

    rules = {'other': [('crossed', -2)], ('crossed', 2): [('beside', -1)], ('own', 3): [('beside', -1)]}

    @functools.cache
    def arrived(kind, k):
        if k == 0:
            return dict(own=lambda: [wave], other=lambda: [swap(wave)], beside=lambda: across(wave))[kind]()
        x = arrived("other", k) if kind == "crossed" else arrived(kind, k - 1)
        done = []
        for before, shift in (*rules.get(kind, ()), *rules.get((kind, k), ())):
            most_hops = half - 1 if before in ("other", "crossed") else half
            if 1 <= k + shift <= most_hops:
                done += arrived(before, k + shift)
        if done:
            x = [lax.optimization_barrier((y, *done))[0] for y in x]
        if (kind, k) == ('beside', 1):
            x = [lax.optimization_barrier((y, table))[0] for y in x]
        if kind == "crossed":
            return across(x[0])
        return [hop(y) for y in x]

    units = [[wave_near] + arrived("beside", 0)]
    for k in range(1, half):
        units += [arrived("own", k) + arrived("beside", k), arrived("other", k) + arrived("crossed", k)]
    units.append(arrived("own", half) + arrived("beside", half))

    block_shape = (op_size, rows, size)
    blocks_out = jax.ShapeDtypeStruct((asked,) + block_shape, jnp.bfloat16)
    block_sems = [pltpu.SemaphoreType.DMA((asked,)), pltpu.SemaphoreType.DMA]

    def flat(low, high, ties=()):
        arrays = [x for unit in units[low:high] for x in unit]
        tied = [x for kind, k in ties for x in arrived(kind, k)]
        return arrays[:-1] + [lax.optimization_barrier((arrays[-1], *tied))[0]] if tied else arrays

    their_table = swap(table)

    def gather(low, high, arrays):
        slots = min(asked, (high - low) * most)
        (sent,) = call(
            functools.partial(sent_kernel, sizes, low, high),
            "sent",
            [their_table] + arrays,
            [jax.ShapeDtypeStruct((slots,) + block_shape, jnp.bfloat16)],
            [pltpu.SemaphoreType.DMA((slots,)), pltpu.SemaphoreType.DMA],
        )
        return swap(sent)

    first_received = gather(0, early, flat(0, early, (('crossed', 2),)))
    operators_out = [jax.ShapeDtypeStruct(x.shape, jnp.bfloat16) for x in (left_ops, right_ops)]
    lefts, rights, blocks = call(
        functools.partial(load_kernel, sizes, early),
        "load",
        [table, left_ops, right_ops] + flat(0, early, ()),
        operators_out + [blocks_out],
        [pltpu.SemaphoreType.DMA((asked,)), pltpu.SemaphoreType.DMA((3,))],
    )
    late = flat(early, chips)
    received = gather(early, chips, [lax.optimization_barrier((late[0], lefts))[0]] + late[1:])
    operands = [table, first_received] + late + [blocks]
    (blocks,) = call(
        functools.partial(fill_kernel, sizes, early),
        "fill",
        operands,
        [blocks_out],
        block_sems,
        [whole] + [apart] * (len(late) + 1) + [whole],
        {len(operands) - 1: 0},
    )

    results, held = [], []
    parts = [targets - 2, 2]
    for first, count in zip([sum(parts[:i]) for i in range(len(parts))], parts):
        keep, send, blocks = call(
            functools.partial(product_kernel, sizes, early, first, count),
            "product",
            [table, received, lefts, rights, blocks],
            [
                jax.ShapeDtypeStruct((count, rows, size), jnp.float32),
                jax.ShapeDtypeStruct((op_size - 1, count, rows, size), jnp.bfloat16),
                blocks_out,
            ],
            block_sems,
            [whole, apart] + [whole] * 3,
            {4: 2},
            4 * count * terms * size**3,
        )
        for k in range(1, op_size):
            turn = [(p, (p + k) % op_size) for p in range(op_size)]
            part = lax.ppermute(send[k - 1], "op", turn)
            if first + count < targets:
                part = pl.pallas_call(
                    held_kernel,
                    name="held",
                    in_specs=[apart],
                    out_specs=apart,
                    out_shape=jax.ShapeDtypeStruct(part.shape, part.dtype),
                    input_output_aliases={0: 0},
                    cost_estimate=pl.CostEstimate(
                        flops=0, bytes_accessed=100 * part.size, transcendentals=0
                    ),
                )(part)
                held.append(part)
            elif held:
                keep = lax.optimization_barrier((keep, *held))[0]
            keep = keep + part.astype(jnp.float32)
        results.append(keep.astype(jnp.bfloat16))
    return jnp.concatenate(results)


def solution(mesh):
    sec_size, op_size = mesh.shape["sec"], mesh.shape["op"]
    split = Mesh(mesh.devices.reshape(sec_size // 2, 2, op_size), ("chip", "core", "op"))
    sec = ("chip", "core")
    in_specs = (
        P(sec, "op", None),
        P(sec, "op", None, None),
        P(sec, "op", None, None),
        P(sec, None),
        P(sec, None),
        P("op"),
    )
    out_specs = P(sec, "op", None)
    return jax.shard_map(shards, mesh=split, in_specs=in_specs, out_specs=out_specs, check_vma=False)
```

profile of v0, /device:TPU:0, one launch (start us, length us, event | category | flops | bytes accessed | tf_op | source)
XLA Modules:
  0.0 78.0 jit_solution(5127355590223210770)
XLA Ops:
  0.5 2.5 %collective-permute-start.3 = (bf16[6,128,256]{2,1,0:T(8,128)(2,1)}, bf16[6,128,256]{2,1,0:T(8,128)(2,1)S(1)}, u32[]{:S(2)}, u32[]{:S(2)}) collective-permute-start(bf16[6,128,256]{2,1,0:T(8,128)(2,1)} %wave.1), channel_id=1, source_target_pairs={{1,0},{0,1},{3,2},{2,3},{5,4},{4,5},{7,6},{6,7},{9,8},{8,9},{11,10... | collective-permute-start | bytes 1179656 | tf_op jit(solution)/shard_map/ppermute | solution.py:241
  2.9 2.0 %collective-permute-start.8 = (bf16[6,128,256]{2,1,0:T(8,128)(2,1)S(1)}, bf16[6,128,256]{2,1,0:T(8,128)(2,1)S(1)}, u32[]{:S(2)}, u32[]{:S(2)}) collective-permute-start(bf16[6,128,256]{2,1,0:T(8,128)(2,1)S(1)} %collective-permute-done.7), channel_id=1, source_target_pairs={{0,8},{2,6},{8,16},{10,2},{16,24},{18,10},{24,28},{26,18},{28,20},... | collective-permute-start | bytes 1179656 | tf_op jit(solution)/shard_map/ppermute | solution.py:234
  9.6 2.9 %table.1 = (s32[8,128]{1,0:T(8,128)S(1)}, bf16[6,128,256]{2,1,0:T(8,128)(2,1)S(1)}) custom-call(s32[6,5]{1,0:T(8,128)S(1)} %copy-done.1, s32[6,5]{1,0:T(8,128)S(1)} %copy-done.2, s32[8]{0:T(128)S(1)} %copy-done.3, bf16[6,128,256]{2,1,0:T(8,128)(2,1)S(1)} %copy-done), custom_call_target="tpu_custom_call" | custom-call | bytes 395264 | tf_op jit(solution)/shard_map/table/pallas_call | solution.py:249
  12.9 1.8 %collective-permute-start.4 = (bf16[6,128,256]{2,1,0:T(8,128)(2,1)S(1)}, bf16[6,128,256]{2,1,0:T(8,128)(2,1)S(1)}, u32[]{:S(2)}, u32[]{:S(2)}) collective-permute-start(bf16[6,128,256]{2,1,0:T(8,128)(2,1)S(1)} %collective-permute-done.3.refs_1_), channel_id=1, source_target_pairs={{0,8},{2,6},{8,16},{10,2},{16,24},{18,10},{24,28},{26,18},{28,20},... | collective-permute-start | bytes 1179656 | tf_op jit(solution)/shard_map/ppermute | solution.py:234
  14.8 1.6 %collective-permute-start.10 = (bf16[6,128,256]{2,1,0:T(8,128)(2,1)S(1)}, bf16[6,128,256]{2,1,0:T(8,128)(2,1)S(1)}, u32[]{:S(2)}, u32[]{:S(2)}) collective-permute-start(bf16[6,128,256]{2,1,0:T(8,128)(2,1)S(1)} %collective-permute-done.8.refs_4_), channel_id=1, source_target_pairs={{0,8},{2,6},{8,16},{10,2},{16,24},{18,10},{24,28},{26,18},{28,20},... | collective-permute-start | bytes 1179656 | tf_op jit(solution)/shard_map/ppermute | solution.py:234
  17.8 1.6 %collective-permute-start.2 = (bf16[6,128,256]{2,1,0:T(8,128)(2,1)S(1)}, bf16[6,128,256]{2,1,0:T(8,128)(2,1)S(1)}, u32[]{:S(2)}, u32[]{:S(2)}) collective-permute-start(bf16[6,128,256]{2,1,0:T(8,128)(2,1)S(1)} %collective-permute-done.1.refs_2_), channel_id=1, source_target_pairs={{0,8},{2,6},{8,16},{10,2},{16,24},{18,10},{24,28},{26,18},{28,20},... | collective-permute-start | bytes 1179656 | tf_op jit(solution)/shard_map/ppermute | solution.py:234
  20.7 1.8 %collective-permute-start.5 = (bf16[6,128,256]{2,1,0:T(8,128)(2,1)S(1)}, bf16[6,128,256]{2,1,0:T(8,128)(2,1)S(1)}, u32[]{:S(2)}, u32[]{:S(2)}) collective-permute-start(bf16[6,128,256]{2,1,0:T(8,128)(2,1)S(1)} %collective-permute-done.4.refs_3_), channel_id=1, source_target_pairs={{0,8},{2,6},{8,16},{10,2},{16,24},{18,10},{24,28},{26,18},{28,20},... | collective-permute-start | bytes 1179656 | tf_op jit(solution)/shard_map/ppermute | solution.py:234
  22.5 2.4 %collective-permute-done.10.refs_8_ = bf16[6,128,256]{2,1,0:T(8,128)(2,1)S(1)} collective-permute-done((bf16[6,128,256]{2,1,0:T(8,128)(2,1)S(1)}, bf16[6,128,256]{2,1,0:T(8,128)(2,1)S(1)}, u32[]{:S(2)}, u32[]{:S(2)}) %collective-permute-start.10) | collective-permute-done | bytes 393248 | tf_op jit(solution)/shard_map/ppermute | solution.py:234
  24.9 1.7 %collective-permute-start.11 = (bf16[6,128,256]{2,1,0:T(8,128)(2,1)S(1)}, bf16[6,128,256]{2,1,0:T(8,128)(2,1)S(1)}, u32[]{:S(2)}, u32[]{:S(2)}) collective-permute-start(bf16[6,128,256]{2,1,0:T(8,128)(2,1)S(1)} %collective-permute-done.10.refs_8_), channel_id=1, source_target_pairs={{1,0},{0,1},{3,2},{2,3},{5,4},{4,5},{7,6},{6,7},{9,8},{8,9},{11,10... | collective-permute-start | bytes 1179656 | tf_op jit(solution)/shard_map/ppermute | solution.py:241
  26.7 1.6 %collective-permute-start.13 = (bf16[6,128,256]{2,1,0:T(8,128)(2,1)S(1)}, bf16[6,128,256]{2,1,0:T(8,128)(2,1)S(1)}, u32[]{:S(2)}, u32[]{:S(2)}) collective-permute-start(bf16[6,128,256]{2,1,0:T(8,128)(2,1)S(1)} %collective-permute-done.10.refs_8_), channel_id=1, source_target_pairs={{0,8},{2,6},{8,16},{10,2},{16,24},{18,10},{24,28},{26,18},{28,20},... | collective-permute-start | bytes 1179656 | tf_op jit(solution)/shard_map/ppermute | solution.py:234
  29.1 4.2 %collective-permute-done.5.refs_7_ = bf16[6,128,256]{2,1,0:T(8,128)(2,1)S(1)} collective-permute-done((bf16[6,128,256]{2,1,0:T(8,128)(2,1)S(1)}, bf16[6,128,256]{2,1,0:T(8,128)(2,1)S(1)}, u32[]{:S(2)}, u32[]{:S(2)}) %collective-permute-start.5) | collective-permute-done | bytes 393248 | tf_op jit(solution)/shard_map/ppermute | solution.py:234
  33.4 1.8 %collective-permute-start.6 = (bf16[6,128,256]{2,1,0:T(8,128)(2,1)S(1)}, bf16[6,128,256]{2,1,0:T(8,128)(2,1)S(1)}, u32[]{:S(2)}, u32[]{:S(2)}) collective-permute-start(bf16[6,128,256]{2,1,0:T(8,128)(2,1)S(1)} %collective-permute-done.2.refs_6_), channel_id=1, source_target_pairs={{0,8},{2,6},{8,16},{10,2},{16,24},{18,10},{24,28},{26,18},{28,20},... | collective-permute-start | bytes 1179656 | tf_op jit(solution)/shard_map/ppermute | solution.py:234
  36.8 2.5 %sent.3 = bf16[15,2,128,256]{3,2,1,0:T(8,128)(2,1)S(1)} custom-call(s32[8,128]{1,0:T(8,128)S(1)} %collective-permute-done.asked_in, bf16[6,128,256]{2,1,0:T(8,128)(2,1)S(1)} %get-tuple-element.25.refs_0_, bf16[6,128,256]{2,1,0:T(8,128)(2,1)S(1)} %collective-permute-done.3.refs_1_, bf16[6,128,256]{2,1,0:T(8,128)(2,1)S(1)} %collective-permute-done.1.refs_2_, ...), custom_call_target="tpu_custom_call" | custom-call | bytes 1966080 | tf_op jit(solution)/shard_map/sent/pallas_call | solution.py:249
  41.8 1.8 %collective-permute-start.15 = (bf16[6,128,256]{2,1,0:T(8,128)(2,1)S(1)}, bf16[6,128,256]{2,1,0:T(8,128)(2,1)S(1)}, u32[]{:S(2)}, u32[]{:S(2)}) collective-permute-start(bf16[6,128,256]{2,1,0:T(8,128)(2,1)S(1)} %collective-permute-done.6.refs_0_), channel_id=1, source_target_pairs={{0,8},{2,6},{8,16},{10,2},{16,24},{18,10},{24,28},{26,18},{28,20},... | collective-permute-start | bytes 1179656 | tf_op jit(solution)/shard_map/ppermute | solution.py:234
  43.6 2.4 %collective-permute-done.12.refs_1_ = bf16[6,128,256]{2,1,0:T(8,128)(2,1)S(1)} collective-permute-done((bf16[6,128,256]{2,1,0:T(8,128)(2,1)S(1)}, bf16[6,128,256]{2,1,0:T(8,128)(2,1)S(1)}, u32[]{:S(2)}, u32[]{:S(2)}) %collective-permute-start.12) | collective-permute-done | bytes 393248 | tf_op jit(solution)/shard_map/ppermute | solution.py:234
  46.0 1.8 %collective-permute-start.16 = (bf16[6,128,256]{2,1,0:T(8,128)(2,1)S(1)}, bf16[6,128,256]{2,1,0:T(8,128)(2,1)S(1)}, u32[]{:S(2)}, u32[]{:S(2)}) collective-permute-start(bf16[6,128,256]{2,1,0:T(8,128)(2,1)S(1)} %collective-permute-done.12.refs_1_), channel_id=1, source_target_pairs={{0,8},{2,6},{8,16},{10,2},{16,24},{18,10},{24,28},{26,18},{28,20},... | collective-permute-start | bytes 1179656 | tf_op jit(solution)/shard_map/ppermute | solution.py:234
  47.8 4.9 %load.1 = (bf16[6,8,256,256]{3,2,1,0:T(8,128)(2,1)S(1)}, bf16[6,8,256,256]{3,2,1,0:T(8,128)(2,1)S(1)}, bf16[30,2,128,256]{3,2,1,0:T(8,128)(2,1)S(1)}) custom-call(s32[8,128]{1,0:T(8,128)S(1)} %get-tuple-element.22.table_in, bf16[6,8,256,256]{3,2,1,0:T(8,128)(2,1)} %left.1, bf16[6,8,256,256]{3,2,1,0:T(8,128)(2,1)} %right.1, ...), custom_call_target="tpu_custom_call" | custom-call | bytes 16515072 | tf_op jit(solution)/shard_map/load/pallas_call | solution.py:249
  52.8 1.7 %collective-permute-done.16.refs_5_ = bf16[6,128,256]{2,1,0:T(8,128)(2,1)S(1)} collective-permute-done((bf16[6,128,256]{2,1,0:T(8,128)(2,1)S(1)}, bf16[6,128,256]{2,1,0:T(8,128)(2,1)S(1)}, u32[]{:S(2)}, u32[]{:S(2)}) %collective-permute-start.16) | collective-permute-done | bytes 393248 | tf_op jit(solution)/shard_map/ppermute | solution.py:234
  54.4 1.9 %sent.2 = bf16[9,2,128,256]{3,2,1,0:T(8,128)(2,1)S(1)} custom-call(s32[8,128]{1,0:T(8,128)S(1)} %collective-permute-done.asked_in, bf16[6,128,256]{2,1,0:T(8,128)(2,1)S(1)} %collective-permute-done.6.refs_0_, bf16[6,128,256]{2,1,0:T(8,128)(2,1)S(1)} %collective-permute-done.12.refs_1_, bf16[6,128,256]{2,1,0:T(8,128)(2,1)S(1)} %collective-permute-done.13.refs_2_, ...), custom_call_target="tpu_custom_call" | custom-call | bytes 1179648 | tf_op jit(solution)/shard_map/sent/pallas_call | solution.py:249
  56.4 3.8 %fill.1._ = bf16[30,2,128,256]{3,2,1,0:T(8,128)(2,1)S(1)} custom-call(s32[8,128]{1,0:T(8,128)S(1)} %get-tuple-element.22.table_in, bf16[15,2,128,256]{3,2,1,0:T(8,128)(2,1)S(1)} %collective-permute-done.18.received, bf16[6,128,256]{2,1,0:T(8,128)(2,1)S(1)} %collective-permute-done.6.refs_0_, ...), custom_call_target="tpu_custom_call", output_to_operand_aliasing={{}: (8, {})} | custom-call | bytes 3932160 | tf_op jit(solution)/shard_map/fill/pallas_call | solution.py:249
  60.2 5.4 %product.2 = (f32[4,128,256]{2,1,0:T(8,128)S(1)}, bf16[1,4,128,256]{3,2,1,0:T(8,128)(2,1)S(1)}, bf16[30,2,128,256]{3,2,1,0:T(8,128)(2,1)S(1)}) custom-call(s32[8,128]{1,0:T(8,128)S(1)} %get-tuple-element.22.table_in, bf16[9,2,128,256]{3,2,1,0:T(8,128)(2,1)S(1)} %collective-permute-done.17.received, ...), custom_call_target="tpu_custom_call", output_to_operand_aliasing={{2}: (4, {})} | custom-call | flops 2147483648 | bytes 4456448 | tf_op jit(solution)/shard_map/product/pallas_call | solution.py:249
  65.5 1.8 %collective-permute-start.19 = (bf16[4,128,256]{2,1,0:T(8,128)(2,1)S(1)}, bf16[4,128,256]{2,1,0:T(8,128)(2,1)S(1)}, u32[]{:S(2)}, u32[]{:S(2)}) collective-permute-start(bf16[4,128,256]{2,1,0:T(8,128)(2,1)S(1)} %bitcast.2), channel_id=1, source_target_pairs={{0,1},{1,0},{2,3},{3,2},{4,5},{5,4},{6,7},{7,6},{8,9},{9,8},{10,11... | collective-permute-start | bytes 786440 | tf_op jit(solution)/shard_map/ppermute | solution.py:364
  67.4 2.6 %product.3 = (f32[2,128,256]{2,1,0:T(8,128)S(1)}, bf16[1,2,128,256]{3,2,1,0:T(8,128)(2,1)S(1)}, bf16[30,2,128,256]{3,2,1,0:T(8,128)(2,1)S(1)}) custom-call(s32[8,128]{1,0:T(8,128)S(1)} %get-tuple-element.22.table_in, bf16[9,2,128,256]{3,2,1,0:T(8,128)(2,1)S(1)} %collective-permute-done.17.received, ...), custom_call_target="tpu_custom_call", output_to_operand_aliasing={{2}: (4, {})} | custom-call | flops 1073741824 | bytes 4194304 | tf_op jit(solution)/shard_map/product/pallas_call | solution.py:249
  70.3 4.4 %collective-permute-done.19.source = bf16[4,128,256]{2,1,0:T(8,128)(2,1)S(1)} collective-permute-done((bf16[4,128,256]{2,1,0:T(8,128)(2,1)S(1)}, bf16[4,128,256]{2,1,0:T(8,128)(2,1)S(1)}, u32[]{:S(2)}, u32[]{:S(2)}) %collective-permute-start.19) | collective-permute-done | bytes 262176 | tf_op jit(solution)/shard_map/ppermute | solution.py:364
  (39 shorter events, 17.0 us)
Async XLA Ops:
  0.0 2.9 %collective-permute-start.7 = (bf16[6,128,256]{2,1,0:T(8,128)(2,1)}, bf16[6,128,256]{2,1,0:T(8,128)(2,1)S(1)}, u32[]{:S(2)}, u32[]{:S(2)}) collective-permute-start(bf16[6,128,256]{2,1,0:T(8,128)(2,1)} %wave.1), channel_id=1, source_target_pairs={{0,2},{2,0},{1,3},{3,1},{4,6},{6,4},{5,7},{7,5},{8,10},{10,8},{9,1... | collective-permute-start | bytes 1179656 | tf_op jit(solution)/shard_map/ppermute | solution.py:237
  0.5 12.5 %collective-permute-start.3 = (bf16[6,128,256]{2,1,0:T(8,128)(2,1)}, bf16[6,128,256]{2,1,0:T(8,128)(2,1)S(1)}, u32[]{:S(2)}, u32[]{:S(2)}) collective-permute-start(bf16[6,128,256]{2,1,0:T(8,128)(2,1)} %wave.1), channel_id=1, source_target_pairs={{1,0},{0,1},{3,2},{2,3},{5,4},{4,5},{7,6},{6,7},{9,8},{8,9},{11,10... | collective-permute-start | bytes 1179656 | tf_op jit(solution)/shard_map/ppermute | solution.py:241
  2.9 11.8 %collective-permute-start.8 = (bf16[6,128,256]{2,1,0:T(8,128)(2,1)S(1)}, bf16[6,128,256]{2,1,0:T(8,128)(2,1)S(1)}, u32[]{:S(2)}, u32[]{:S(2)}) collective-permute-start(bf16[6,128,256]{2,1,0:T(8,128)(2,1)S(1)} %collective-permute-done.7), channel_id=1, source_target_pairs={{0,8},{2,6},{8,16},{10,2},{16,24},{18,10},{24,28},{26,18},{28,20},... | collective-permute-start | bytes 1179656 | tf_op jit(solution)/shard_map/ppermute | solution.py:234
  5.0 12.9 %collective-permute-start.1 = (bf16[6,128,256]{2,1,0:T(8,128)(2,1)}, bf16[6,128,256]{2,1,0:T(8,128)(2,1)S(1)}, u32[]{:S(2)}, u32[]{:S(2)}) collective-permute-start(bf16[6,128,256]{2,1,0:T(8,128)(2,1)} %wave.1), channel_id=1, source_target_pairs={{0,8},{2,6},{8,16},{10,2},{16,24},{18,10},{24,28},{26,18},{28,20},... | collective-permute-start | bytes 1179656 | tf_op jit(solution)/shard_map/ppermute | solution.py:234
  6.5 1.0 %copy-start = (bf16[6,128,256]{2,1,0:T(8,128)(2,1)S(1)}, bf16[6,128,256]{2,1,0:T(8,128)(2,1)}, u32[]{:S(2)}) copy-start(bf16[6,128,256]{2,1,0:T(8,128)(2,1)} %wave.1) | copy-start | bytes 1179652
  7.6 0.7 copy-start.1
  12.9 7.8 %collective-permute-start.4 = (bf16[6,128,256]{2,1,0:T(8,128)(2,1)S(1)}, bf16[6,128,256]{2,1,0:T(8,128)(2,1)S(1)}, u32[]{:S(2)}, u32[]{:S(2)}) collective-permute-start(bf16[6,128,256]{2,1,0:T(8,128)(2,1)S(1)} %collective-permute-done.3.refs_1_), channel_id=1, source_target_pairs={{0,8},{2,6},{8,16},{10,2},{16,24},{18,10},{24,28},{26,18},{28,20},... | collective-permute-start | bytes 1179656 | tf_op jit(solution)/shard_map/ppermute | solution.py:234
  14.8 10.2 %collective-permute-start.10 = (bf16[6,128,256]{2,1,0:T(8,128)(2,1)S(1)}, bf16[6,128,256]{2,1,0:T(8,128)(2,1)S(1)}, u32[]{:S(2)}, u32[]{:S(2)}) collective-permute-start(bf16[6,128,256]{2,1,0:T(8,128)(2,1)S(1)} %collective-permute-done.8.refs_4_), channel_id=1, source_target_pairs={{0,8},{2,6},{8,16},{10,2},{16,24},{18,10},{24,28},{26,18},{28,20},... | collective-permute-start | bytes 1179656 | tf_op jit(solution)/shard_map/ppermute | solution.py:234
  16.3 10.3 %collective-permute-start.9 = (bf16[6,128,256]{2,1,0:T(8,128)(2,1)S(1)}, bf16[6,128,256]{2,1,0:T(8,128)(2,1)S(1)}, u32[]{:S(2)}, u32[]{:S(2)}) collective-permute-start(bf16[6,128,256]{2,1,0:T(8,128)(2,1)S(1)} %collective-permute-done.8.refs_4_), channel_id=1, source_target_pairs={{1,0},{0,1},{3,2},{2,3},{5,4},{4,5},{7,6},{6,7},{9,8},{8,9},{11,10... | collective-permute-start | bytes 1179656 | tf_op jit(solution)/shard_map/ppermute | solution.py:241
  17.8 11.3 %collective-permute-start.2 = (bf16[6,128,256]{2,1,0:T(8,128)(2,1)S(1)}, bf16[6,128,256]{2,1,0:T(8,128)(2,1)S(1)}, u32[]{:S(2)}, u32[]{:S(2)}) collective-permute-start(bf16[6,128,256]{2,1,0:T(8,128)(2,1)S(1)} %collective-permute-done.1.refs_2_), channel_id=1, source_target_pairs={{0,8},{2,6},{8,16},{10,2},{16,24},{18,10},{24,28},{26,18},{28,20},... | collective-permute-start | bytes 1179656 | tf_op jit(solution)/shard_map/ppermute | solution.py:234
  20.7 12.6 %collective-permute-start.5 = (bf16[6,128,256]{2,1,0:T(8,128)(2,1)S(1)}, bf16[6,128,256]{2,1,0:T(8,128)(2,1)S(1)}, u32[]{:S(2)}, u32[]{:S(2)}) collective-permute-start(bf16[6,128,256]{2,1,0:T(8,128)(2,1)S(1)} %collective-permute-done.4.refs_3_), channel_id=1, source_target_pairs={{0,8},{2,6},{8,16},{10,2},{16,24},{18,10},{24,28},{26,18},{28,20},... | collective-permute-start | bytes 1179656 | tf_op jit(solution)/shard_map/ppermute | solution.py:234
  24.9 11.8 %collective-permute-start.11 = (bf16[6,128,256]{2,1,0:T(8,128)(2,1)S(1)}, bf16[6,128,256]{2,1,0:T(8,128)(2,1)S(1)}, u32[]{:S(2)}, u32[]{:S(2)}) collective-permute-start(bf16[6,128,256]{2,1,0:T(8,128)(2,1)S(1)} %collective-permute-done.10.refs_8_), channel_id=1, source_target_pairs={{1,0},{0,1},{3,2},{2,3},{5,4},{4,5},{7,6},{6,7},{9,8},{8,9},{11,10... | collective-permute-start | bytes 1179656 | tf_op jit(solution)/shard_map/ppermute | solution.py:241
  26.7 10.1 %collective-permute-start = (s32[8,128]{1,0:T(8,128)S(1)}, s32[8,128]{1,0:T(8,128)S(1)}, u32[]{:S(2)}, u32[]{:S(2)}) collective-permute-start(s32[8,128]{1,0:T(8,128)S(1)} %get-tuple-element.22.table_in), channel_id=1, source_target_pairs={{0,2},{2,0},{1,3},{3,1},{4,6},{6,4},{5,7},{7,5},{8,10},{10,8},{9,1... | collective-permute-start | bytes 12296 | tf_op jit(solution)/shard_map/ppermute | solution.py:237
  26.7 12.7 %collective-permute-start.13 = (bf16[6,128,256]{2,1,0:T(8,128)(2,1)S(1)}, bf16[6,128,256]{2,1,0:T(8,128)(2,1)S(1)}, u32[]{:S(2)}, u32[]{:S(2)}) collective-permute-start(bf16[6,128,256]{2,1,0:T(8,128)(2,1)S(1)} %collective-permute-done.10.refs_8_), channel_id=1, source_target_pairs={{0,8},{2,6},{8,16},{10,2},{16,24},{18,10},{24,28},{26,18},{28,20},... | collective-permute-start | bytes 1179656 | tf_op jit(solution)/shard_map/ppermute | solution.py:234
  33.4 8.4 %collective-permute-start.6 = (bf16[6,128,256]{2,1,0:T(8,128)(2,1)S(1)}, bf16[6,128,256]{2,1,0:T(8,128)(2,1)S(1)}, u32[]{:S(2)}, u32[]{:S(2)}) collective-permute-start(bf16[6,128,256]{2,1,0:T(8,128)(2,1)S(1)} %collective-permute-done.2.refs_6_), channel_id=1, source_target_pairs={{0,8},{2,6},{8,16},{10,2},{16,24},{18,10},{24,28},{26,18},{28,20},... | collective-permute-start | bytes 1179656 | tf_op jit(solution)/shard_map/ppermute | solution.py:234
  35.2 10.8 %collective-permute-start.12 = (bf16[6,128,256]{2,1,0:T(8,128)(2,1)S(1)}, bf16[6,128,256]{2,1,0:T(8,128)(2,1)S(1)}, u32[]{:S(2)}, u32[]{:S(2)}) collective-permute-start(bf16[6,128,256]{2,1,0:T(8,128)(2,1)S(1)} %collective-permute-done.5.refs_7_), channel_id=1, source_target_pairs={{0,8},{2,6},{8,16},{10,2},{16,24},{18,10},{24,28},{26,18},{28,20},... | collective-permute-start | bytes 1179656 | tf_op jit(solution)/shard_map/ppermute | solution.py:234
  39.3 17.1 %collective-permute-start.18 = (bf16[15,2,128,256]{3,2,1,0:T(8,128)(2,1)S(1)}, bf16[15,2,128,256]{3,2,1,0:T(8,128)(2,1)S(1)}, u32[]{:S(2)}, u32[]{:S(2)}) collective-permute-start(bf16[15,2,128,256]{3,2,1,0:T(8,128)(2,1)S(1)} %sent.3), channel_id=1, source_target_pairs={{0,2},{2,0},{1,3},{3,1},{4,6},{6,4},{5,7},{7,5},{8,10},{10,8},{9,1... | collective-permute-start | bytes 5898248 | tf_op jit(solution)/shard_map/ppermute | solution.py:237
  39.4 13.4 %collective-permute-start.14 = (bf16[6,128,256]{2,1,0:T(8,128)(2,1)S(1)}, bf16[6,128,256]{2,1,0:T(8,128)(2,1)S(1)}, u32[]{:S(2)}, u32[]{:S(2)}) collective-permute-start(bf16[6,128,256]{2,1,0:T(8,128)(2,1)S(1)} %collective-permute-done.13.refs_2_), channel_id=1, source_target_pairs={{1,0},{0,1},{3,2},{2,3},{5,4},{4,5},{7,6},{6,7},{9,8},{8,9},{11,10... | collective-permute-start | bytes 1179656 | tf_op jit(solution)/shard_map/ppermute | solution.py:241
  41.8 11.0 %collective-permute-start.15 = (bf16[6,128,256]{2,1,0:T(8,128)(2,1)S(1)}, bf16[6,128,256]{2,1,0:T(8,128)(2,1)S(1)}, u32[]{:S(2)}, u32[]{:S(2)}) collective-permute-start(bf16[6,128,256]{2,1,0:T(8,128)(2,1)S(1)} %collective-permute-done.6.refs_0_), channel_id=1, source_target_pairs={{0,8},{2,6},{8,16},{10,2},{16,24},{18,10},{24,28},{26,18},{28,20},... | collective-permute-start | bytes 1179656 | tf_op jit(solution)/shard_map/ppermute | solution.py:234
  46.0 8.4 %collective-permute-start.16 = (bf16[6,128,256]{2,1,0:T(8,128)(2,1)S(1)}, bf16[6,128,256]{2,1,0:T(8,128)(2,1)S(1)}, u32[]{:S(2)}, u32[]{:S(2)}) collective-permute-start(bf16[6,128,256]{2,1,0:T(8,128)(2,1)S(1)} %collective-permute-done.12.refs_1_), channel_id=1, source_target_pairs={{0,8},{2,6},{8,16},{10,2},{16,24},{18,10},{24,28},{26,18},{28,20},... | collective-permute-start | bytes 1179656 | tf_op jit(solution)/shard_map/ppermute | solution.py:234
  56.3 3.9 %collective-permute-start.17 = (bf16[9,2,128,256]{3,2,1,0:T(8,128)(2,1)S(1)}, bf16[9,2,128,256]{3,2,1,0:T(8,128)(2,1)S(1)}, u32[]{:S(2)}, u32[]{:S(2)}) collective-permute-start(bf16[9,2,128,256]{3,2,1,0:T(8,128)(2,1)S(1)} %sent.2), channel_id=1, source_target_pairs={{0,2},{2,0},{1,3},{3,1},{4,6},{6,4},{5,7},{7,5},{8,10},{10,8},{9,1... | collective-permute-start | bytes 3538952 | tf_op jit(solution)/shard_map/ppermute | solution.py:237
  65.5 9.2 %collective-permute-start.19 = (bf16[4,128,256]{2,1,0:T(8,128)(2,1)S(1)}, bf16[4,128,256]{2,1,0:T(8,128)(2,1)S(1)}, u32[]{:S(2)}, u32[]{:S(2)}) collective-permute-start(bf16[4,128,256]{2,1,0:T(8,128)(2,1)S(1)} %bitcast.2), channel_id=1, source_target_pairs={{0,1},{1,0},{2,3},{3,2},{4,5},{5,4},{6,7},{7,6},{8,9},{9,8},{10,11... | collective-permute-start | bytes 786440 | tf_op jit(solution)/shard_map/ppermute | solution.py:364
  69.9 7.2 %collective-permute-start.20 = (bf16[2,128,256]{2,1,0:T(8,128)(2,1)S(1)}, bf16[2,128,256]{2,1,0:T(8,128)(2,1)S(1)}, u32[]{:S(2)}, u32[]{:S(2)}) collective-permute-start(bf16[2,128,256]{2,1,0:T(8,128)(2,1)S(1)} %bitcast.3), channel_id=1, source_target_pairs={{0,1},{1,0},{2,3},{3,2},{4,5},{5,4},{6,7},{7,6},{8,9},{9,8},{10,11... | collective-permute-start | bytes 393224 | tf_op jit(solution)/shard_map/ppermute | solution.py:364
  74.7 0.7 copy-start.4
  (2 other events, 1.3 us)
where the time goes:
time: 78.2 us; the launch traced here: 78 us
  starting transfers between devices  29.1 us (37%)
  Pallas kernels  23.8 us (30%)
  waiting for transfers between devices  19.3 us (25%)
  local copies, waits for them, and re-layouts  3.76 us (5%)
  other arithmetic  1.82 us (2%)
    pallas_call x7, Pallas kernels, call(): pl.pallas_call(kernel, name=name, in_specs=specs or [whole] + [apart] * (...  23.8 us
    ppermute x11, starting transfers between devices, hop(): return lax.ppermute(x, ('chip', 'core'), pairs)  19 us
    ppermute x11, waiting for transfers between devices, hop(): return lax.ppermute(x, ('chip', 'core'), pairs)  13.7 us
    ppermute x4, starting transfers between devices, across(): lax.ppermute(x, 'op', [((q + j) % op_size, q) for q in range(op_size)])  7.28 us
    ppermute x2, waiting for transfers between devices, shards(): part = lax.ppermute(send[k - 1], 'op', turn)  5.15 us
    unnamed x10, local copies, waits for them, and re-layouts  3.76 us
    ppermute x2, starting transfers between devices, shards(): part = lax.ppermute(send[k - 1], 'op', turn)  2.17 us
  transfers between devices with their start and end apart: 21, of which 10 were waited for; matrix products, arithmetic and copies ran while one was open for 1% of the time, Pallas kernels for 24%

commit v1 on v0

--- a/solution.py
+++ b/solution.py
@@ -9,7 +9,7 @@
 
 ORDER, START, SECTOR, CLASS, LATER = range(5)
 TABLE = (8, 128)
-LIMITS = dict(table=4, sent=8, load=32, fill=8, product=24)
+LIMITS = dict(table=4, sent=8, load=30, fill=8, product=24)
 
 
 def ring_position(chip, chips):
@@ -135,18 +135,23 @@
 
 
 def load_kernel(sizes, early, table_in, left, right, *refs):
-    *units, lefts, rights, blocks, table, block_sems, sems = refs
+    targets, terms = sizes[0], sizes[1]
+    *units, lefts, turned, blocks, table, rights, block_sems, right_sems, sems = refs
+    size = lefts.shape[-1]
     loads = [
-        pltpu.make_async_copy(left, lefts, sems.at[0]),
-        pltpu.make_async_copy(right, rights, sems.at[1]),
+        pltpu.make_async_copy(right.at[t], rights.at[t], right_sems.at[t]) for t in range(targets)
     ]
-    for load in loads:
+    left_load = pltpu.make_async_copy(left, lefts, sems.at[0])
+    for load in loads + [left_load]:
         load.start()
-    read_table(table_in, table, sems.at[2])
+    read_table(table_in, table, sems.at[1])
     fetch_own(grouped(units, sizes[3]), 0, table, blocks, block_sems)
+    for t in range(targets):
+        loads[t].wait()
+        for o in range(terms):
+            turned[t, o * size : (o + 1) * size] = rights[t, o].T
     wait_blocks(0, early, table, blocks, block_sems)
-    for load in loads:
-        load.wait()
+    left_load.wait()
 
 
 def fill_kernel(sizes, early, table_in, received, *refs):
@@ -154,8 +159,8 @@
     *units, _, blocks, table, block_sems, sem = refs
     read_table(table_in, table, sem)
     fetch_received(received, chips, chips + early, table, blocks, block_sems)
-    fetch_own(grouped(units, sizes[3]), early, table, blocks, block_sems)
-    wait_blocks(early, chips + early, table, blocks, block_sems)
+    fetch_own(grouped(units, sizes[3]), early + 1, table, blocks, block_sems)
+    wait_blocks(early + 1, chips + early, table, blocks, block_sems)
 
 
 def product_kernel(sizes, early, first, count, table_in, received, lefts, rights, _, *refs):
@@ -192,8 +197,8 @@
             )
         total = lax.dot_general(
             jnp.concatenate(lifted, axis=1),
-            jnp.concatenate([rights[t, o] for o in range(terms)], axis=1),
-            (((1,), (1,)), ((), ())),
+            rights[t],
+            (((1,), (0,)), ((), ())),
             preferred_element_type=jnp.float32,
         )
         for j in range(op_size):
@@ -321,24 +326,33 @@
         return swap(sent)
 
     first_received = gather(0, early, flat(0, early, (('crossed', 2),)))
-    operators_out = [jax.ShapeDtypeStruct(x.shape, jnp.bfloat16) for x in (left_ops, right_ops)]
+    operators_out = [
+        jax.ShapeDtypeStruct(left_ops.shape, jnp.bfloat16),
+        jax.ShapeDtypeStruct((targets, terms * size, size), jnp.bfloat16),
+    ]
     lefts, rights, blocks = call(
-        functools.partial(load_kernel, sizes, early),
+        functools.partial(load_kernel, sizes, early + 1),
         "load",
-        [table, left_ops, right_ops] + flat(0, early, ()),
+        [table, left_ops, right_ops] + flat(0, early + 1, ()),
         operators_out + [blocks_out],
-        [pltpu.SemaphoreType.DMA((asked,)), pltpu.SemaphoreType.DMA((3,))],
+        [
+            pltpu.VMEM(right_ops.shape, jnp.bfloat16),
+            pltpu.SemaphoreType.DMA((asked,)),
+            pltpu.SemaphoreType.DMA((targets,)),
+            pltpu.SemaphoreType.DMA((2,)),
+        ],
     )
     late = flat(early, chips)
     received = gather(early, chips, [lax.optimization_barrier((late[0], lefts))[0]] + late[1:])
-    operands = [table, first_received] + late + [blocks]
+    last = flat(early + 1, chips)
+    operands = [table, first_received] + last + [blocks]
     (blocks,) = call(
         functools.partial(fill_kernel, sizes, early),
         "fill",
         operands,
         [blocks_out],
         block_sems,
-        [whole] + [apart] * (len(late) + 1) + [whole],
+        [whole] + [apart] * (len(last) + 1) + [whole],
         {len(operands) - 1: 0},
     )
 

time: 78.2 us -> 77.7 us (level)
  no operation moved by 1% of the time
where the time goes in v1:
time: 77.7 us
  starting transfers between devices  29.1 us (37%)
  Pallas kernels  24 us (31%)
  waiting for transfers between devices  18.9 us (24%)
  local copies, waits for them, and re-layouts  3.76 us (5%)
  other arithmetic  1.84 us (2%)
    pallas_call x7, Pallas kernels, call(): pl.pallas_call(kernel, name=name, in_specs=specs or [whole] + [apart] * (...  24 us
    ppermute x11, starting transfers between devices, hop(): return lax.ppermute(x, ('chip', 'core'), pairs)  19 us
    ppermute x11, waiting for transfers between devices, hop(): return lax.ppermute(x, ('chip', 'core'), pairs)  12.9 us
    ppermute x4, starting transfers between devices, across(): lax.ppermute(x, 'op', [((q + j) % op_size, q) for q in range(op_size)])  7.28 us
    ppermute x2, waiting for transfers between devices, shards(): part = lax.ppermute(send[k - 1], 'op', turn)  5.49 us
    unnamed x10, local copies, waits for them, and re-layouts  3.76 us
    ppermute x2, starting transfers between devices, shards(): part = lax.ppermute(send[k - 1], 'op', turn)  2.18 us
  transfers between devices with their start and end apart: 21, of which 10 were waited for; matrix products, arithmetic and copies ran while one was open for 1% of the time, Pallas kernels for 24%

profile of v1, /device:TPU:0, one launch (start us, length us, event | category | flops | bytes accessed | tf_op | source)
XLA Modules:
  0.0 77.7 jit_solution(7859179151306707119)
XLA Ops:
  0.5 2.5 %collective-permute-start.3 = (bf16[6,128,256]{2,1,0:T(8,128)(2,1)}, bf16[6,128,256]{2,1,0:T(8,128)(2,1)S(1)}, u32[]{:S(2)}, u32[]{:S(2)}) collective-permute-start(bf16[6,128,256]{2,1,0:T(8,128)(2,1)} %wave.1), channel_id=1, source_target_pairs={{1,0},{0,1},{3,2},{2,3},{5,4},{4,5},{7,6},{6,7},{9,8},{8,9},{11,10... | collective-permute-start | bytes 1179656 | tf_op jit(solution)/shard_map/ppermute | solution.py:246
  2.9 2.0 %collective-permute-start.8 = (bf16[6,128,256]{2,1,0:T(8,128)(2,1)S(1)}, bf16[6,128,256]{2,1,0:T(8,128)(2,1)S(1)}, u32[]{:S(2)}, u32[]{:S(2)}) collective-permute-start(bf16[6,128,256]{2,1,0:T(8,128)(2,1)S(1)} %collective-permute-done.7), channel_id=1, source_target_pairs={{0,8},{2,6},{8,16},{10,2},{16,24},{18,10},{24,28},{26,18},{28,20},... | collective-permute-start | bytes 1179656 | tf_op jit(solution)/shard_map/ppermute | solution.py:239
  5.0 1.6 %collective-permute-start.1 = (bf16[6,128,256]{2,1,0:T(8,128)(2,1)}, bf16[6,128,256]{2,1,0:T(8,128)(2,1)S(1)}, u32[]{:S(2)}, u32[]{:S(2)}) collective-permute-start(bf16[6,128,256]{2,1,0:T(8,128)(2,1)} %wave.1), channel_id=1, source_target_pairs={{0,8},{2,6},{8,16},{10,2},{16,24},{18,10},{24,28},{26,18},{28,20},... | collective-permute-start | bytes 1179656 | tf_op jit(solution)/shard_map/ppermute | solution.py:239
  9.6 2.9 %table.1 = (s32[8,128]{1,0:T(8,128)S(1)}, bf16[6,128,256]{2,1,0:T(8,128)(2,1)S(1)}) custom-call(s32[6,5]{1,0:T(8,128)S(1)} %copy-done.1, s32[6,5]{1,0:T(8,128)S(1)} %copy-done.2, s32[8]{0:T(128)S(1)} %copy-done.3, bf16[6,128,256]{2,1,0:T(8,128)(2,1)S(1)} %copy-done), custom_call_target="tpu_custom_call" | custom-call | bytes 395264 | tf_op jit(solution)/shard_map/table/pallas_call | solution.py:254
  12.9 1.8 %collective-permute-start.4 = (bf16[6,128,256]{2,1,0:T(8,128)(2,1)S(1)}, bf16[6,128,256]{2,1,0:T(8,128)(2,1)S(1)}, u32[]{:S(2)}, u32[]{:S(2)}) collective-permute-start(bf16[6,128,256]{2,1,0:T(8,128)(2,1)S(1)} %collective-permute-done.3.refs_1_), channel_id=1, source_target_pairs={{0,8},{2,6},{8,16},{10,2},{16,24},{18,10},{24,28},{26,18},{28,20},... | collective-permute-start | bytes 1179656 | tf_op jit(solution)/shard_map/ppermute | solution.py:239
  14.8 1.6 %collective-permute-start.10 = (bf16[6,128,256]{2,1,0:T(8,128)(2,1)S(1)}, bf16[6,128,256]{2,1,0:T(8,128)(2,1)S(1)}, u32[]{:S(2)}, u32[]{:S(2)}) collective-permute-start(bf16[6,128,256]{2,1,0:T(8,128)(2,1)S(1)} %collective-permute-done.8.refs_4_), channel_id=1, source_target_pairs={{0,8},{2,6},{8,16},{10,2},{16,24},{18,10},{24,28},{26,18},{28,20},... | collective-permute-start | bytes 1179656 | tf_op jit(solution)/shard_map/ppermute | solution.py:239
  17.8 1.6 %collective-permute-start.2 = (bf16[6,128,256]{2,1,0:T(8,128)(2,1)S(1)}, bf16[6,128,256]{2,1,0:T(8,128)(2,1)S(1)}, u32[]{:S(2)}, u32[]{:S(2)}) collective-permute-start(bf16[6,128,256]{2,1,0:T(8,128)(2,1)S(1)} %collective-permute-done.1.refs_2_), channel_id=1, source_target_pairs={{0,8},{2,6},{8,16},{10,2},{16,24},{18,10},{24,28},{26,18},{28,20},... | collective-permute-start | bytes 1179656 | tf_op jit(solution)/shard_map/ppermute | solution.py:239
  20.7 1.8 %collective-permute-start.5 = (bf16[6,128,256]{2,1,0:T(8,128)(2,1)S(1)}, bf16[6,128,256]{2,1,0:T(8,128)(2,1)S(1)}, u32[]{:S(2)}, u32[]{:S(2)}) collective-permute-start(bf16[6,128,256]{2,1,0:T(8,128)(2,1)S(1)} %collective-permute-done.4.refs_3_), channel_id=1, source_target_pairs={{0,8},{2,6},{8,16},{10,2},{16,24},{18,10},{24,28},{26,18},{28,20},... | collective-permute-start | bytes 1179656 | tf_op jit(solution)/shard_map/ppermute | solution.py:239
  22.5 2.4 %collective-permute-done.10.refs_8_ = bf16[6,128,256]{2,1,0:T(8,128)(2,1)S(1)} collective-permute-done((bf16[6,128,256]{2,1,0:T(8,128)(2,1)S(1)}, bf16[6,128,256]{2,1,0:T(8,128)(2,1)S(1)}, u32[]{:S(2)}, u32[]{:S(2)}) %collective-permute-start.10) | collective-permute-done | bytes 393248 | tf_op jit(solution)/shard_map/ppermute | solution.py:239
  24.9 1.7 %collective-permute-start.11 = (bf16[6,128,256]{2,1,0:T(8,128)(2,1)S(1)}, bf16[6,128,256]{2,1,0:T(8,128)(2,1)S(1)}, u32[]{:S(2)}, u32[]{:S(2)}) collective-permute-start(bf16[6,128,256]{2,1,0:T(8,128)(2,1)S(1)} %collective-permute-done.10.refs_8_), channel_id=1, source_target_pairs={{1,0},{0,1},{3,2},{2,3},{5,4},{4,5},{7,6},{6,7},{9,8},{8,9},{11,10... | collective-permute-start | bytes 1179656 | tf_op jit(solution)/shard_map/ppermute | solution.py:246
  26.7 1.6 %collective-permute-start.13 = (bf16[6,128,256]{2,1,0:T(8,128)(2,1)S(1)}, bf16[6,128,256]{2,1,0:T(8,128)(2,1)S(1)}, u32[]{:S(2)}, u32[]{:S(2)}) collective-permute-start(bf16[6,128,256]{2,1,0:T(8,128)(2,1)S(1)} %collective-permute-done.10.refs_8_), channel_id=1, source_target_pairs={{0,8},{2,6},{8,16},{10,2},{16,24},{18,10},{24,28},{26,18},{28,20},... | collective-permute-start | bytes 1179656 | tf_op jit(solution)/shard_map/ppermute | solution.py:239
  29.1 4.2 %collective-permute-done.5.refs_7_ = bf16[6,128,256]{2,1,0:T(8,128)(2,1)S(1)} collective-permute-done((bf16[6,128,256]{2,1,0:T(8,128)(2,1)S(1)}, bf16[6,128,256]{2,1,0:T(8,128)(2,1)S(1)}, u32[]{:S(2)}, u32[]{:S(2)}) %collective-permute-start.5) | collective-permute-done | bytes 393248 | tf_op jit(solution)/shard_map/ppermute | solution.py:239
  33.4 1.8 %collective-permute-start.6 = (bf16[6,128,256]{2,1,0:T(8,128)(2,1)S(1)}, bf16[6,128,256]{2,1,0:T(8,128)(2,1)S(1)}, u32[]{:S(2)}, u32[]{:S(2)}) collective-permute-start(bf16[6,128,256]{2,1,0:T(8,128)(2,1)S(1)} %collective-permute-done.2.refs_6_), channel_id=1, source_target_pairs={{0,8},{2,6},{8,16},{10,2},{16,24},{18,10},{24,28},{26,18},{28,20},... | collective-permute-start | bytes 1179656 | tf_op jit(solution)/shard_map/ppermute | solution.py:239
  36.8 2.7 %sent.3 = bf16[15,2,128,256]{3,2,1,0:T(8,128)(2,1)S(1)} custom-call(s32[8,128]{1,0:T(8,128)S(1)} %collective-permute-done.asked_in, bf16[6,128,256]{2,1,0:T(8,128)(2,1)S(1)} %get-tuple-element.25.refs_0_, bf16[6,128,256]{2,1,0:T(8,128)(2,1)S(1)} %collective-permute-done.3.refs_1_, bf16[6,128,256]{2,1,0:T(8,128)(2,1)S(1)} %collective-permute-done.1.refs_2_, ...), custom_call_target="tpu_custom_call" | custom-call | bytes 1966080 | tf_op jit(solution)/shard_map/sent/pallas_call | solution.py:254
  41.8 1.8 %collective-permute-start.15 = (bf16[6,128,256]{2,1,0:T(8,128)(2,1)S(1)}, bf16[6,128,256]{2,1,0:T(8,128)(2,1)S(1)}, u32[]{:S(2)}, u32[]{:S(2)}) collective-permute-start(bf16[6,128,256]{2,1,0:T(8,128)(2,1)S(1)} %collective-permute-done.6.refs_10_.refs_0_), channel_id=1, source_target_pairs={{0,8},{2,6},{8,16},{10,2},{16,24},{18,10},{24,28},{26,18},{28,20},... | collective-permute-start | bytes 1179656 | tf_op jit(solution)/shard_map/ppermute | solution.py:239
  43.6 2.4 %collective-permute-done.12.refs_11_.refs_1_ = bf16[6,128,256]{2,1,0:T(8,128)(2,1)S(1)} collective-permute-done((bf16[6,128,256]{2,1,0:T(8,128)(2,1)S(1)}, bf16[6,128,256]{2,1,0:T(8,128)(2,1)S(1)}, u32[]{:S(2)}, u32[]{:S(2)}) %collective-permute-start.12) | collective-permute-done | bytes 393248 | tf_op jit(solution)/shard_map/ppermute | solution.py:239
  46.0 1.8 %collective-permute-start.16 = (bf16[6,128,256]{2,1,0:T(8,128)(2,1)S(1)}, bf16[6,128,256]{2,1,0:T(8,128)(2,1)S(1)}, u32[]{:S(2)}, u32[]{:S(2)}) collective-permute-start(bf16[6,128,256]{2,1,0:T(8,128)(2,1)S(1)} %collective-permute-done.12.refs_11_.refs_1_), channel_id=1, source_target_pairs={{0,8},{2,6},{8,16},{10,2},{16,24},{18,10},{24,28},{26,18},{28,20},... | collective-permute-start | bytes 1179656 | tf_op jit(solution)/shard_map/ppermute | solution.py:239
  47.8 5.5 %load.1 = (bf16[6,8,256,256]{3,2,1,0:T(8,128)(2,1)S(1)}, bf16[6,2048,256]{2,1,0:T(8,128)(2,1)S(1)}, bf16[30,2,128,256]{3,2,1,0:T(8,128)(2,1)S(1)}) custom-call(s32[8,128]{1,0:T(8,128)S(1)} %get-tuple-element.22.table_in, bf16[6,8,256,256]{3,2,1,0:T(8,128)(2,1)} %left.1, bf16[6,8,256,256]{3,2,1,0:T(8,128)(2,1)} %right.1, ...), custom_call_target="tpu_custom_call" | custom-call | bytes 16515072 | tf_op jit(solution)/shard_map/load/pallas_call | solution.py:254
  54.4 2.1 %sent.2 = bf16[9,2,128,256]{3,2,1,0:T(8,128)(2,1)S(1)} custom-call(s32[8,128]{1,0:T(8,128)S(1)} %collective-permute-done.asked_in, bf16[6,128,256]{2,1,0:T(8,128)(2,1)S(1)} %collective-permute-done.6.refs_10_.refs_0_, bf16[6,128,256]{2,1,0:T(8,128)(2,1)S(1)} %collective-permute-done.12.refs_11_.refs_1_, ...), custom_call_target="tpu_custom_call" | custom-call | bytes 1179648 | tf_op jit(solution)/shard_map/sent/pallas_call | solution.py:254
  56.6 3.4 %fill.1._ = bf16[30,2,128,256]{3,2,1,0:T(8,128)(2,1)S(1)} custom-call(s32[8,128]{1,0:T(8,128)S(1)} %get-tuple-element.22.table_in, bf16[15,2,128,256]{3,2,1,0:T(8,128)(2,1)S(1)} %collective-permute-done.18.received, bf16[6,128,256]{2,1,0:T(8,128)(2,1)S(1)} %collective-permute-done.13.refs_2_.refs_0_, ...), custom_call_target="tpu_custom_call", output_to_operand_aliasing={{}: (6, {})} | custom-call | bytes 3932160 | tf_op jit(solution)/shard_map/fill/pallas_call | solution.py:254
  60.0 5.0 %product.2 = (f32[4,128,256]{2,1,0:T(8,128)S(1)}, bf16[1,4,128,256]{3,2,1,0:T(8,128)(2,1)S(1)}, bf16[30,2,128,256]{3,2,1,0:T(8,128)(2,1)S(1)}) custom-call(s32[8,128]{1,0:T(8,128)S(1)} %get-tuple-element.22.table_in, bf16[9,2,128,256]{3,2,1,0:T(8,128)(2,1)S(1)} %collective-permute-done.17.received, ...), custom_call_target="tpu_custom_call", output_to_operand_aliasing={{2}: (4, {})} | custom-call | flops 2147483648 | bytes 4456448 | tf_op jit(solution)/shard_map/product/pallas_call | solution.py:254
  64.9 1.8 %collective-permute-start.19 = (bf16[4,128,256]{2,1,0:T(8,128)(2,1)S(1)}, bf16[4,128,256]{2,1,0:T(8,128)(2,1)S(1)}, u32[]{:S(2)}, u32[]{:S(2)}) collective-permute-start(bf16[4,128,256]{2,1,0:T(8,128)(2,1)S(1)} %bitcast.2), channel_id=1, source_target_pairs={{0,1},{1,0},{2,3},{3,2},{4,5},{5,4},{6,7},{7,6},{8,9},{9,8},{10,11... | collective-permute-start | bytes 786440 | tf_op jit(solution)/shard_map/ppermute | solution.py:378
  66.8 2.5 %product.3 = (f32[2,128,256]{2,1,0:T(8,128)S(1)}, bf16[1,2,128,256]{3,2,1,0:T(8,128)(2,1)S(1)}, bf16[30,2,128,256]{3,2,1,0:T(8,128)(2,1)S(1)}) custom-call(s32[8,128]{1,0:T(8,128)S(1)} %get-tuple-element.22.table_in, bf16[9,2,128,256]{3,2,1,0:T(8,128)(2,1)S(1)} %collective-permute-done.17.received, ...), custom_call_target="tpu_custom_call", output_to_operand_aliasing={{2}: (4, {})} | custom-call | flops 1073741824 | bytes 4194304 | tf_op jit(solution)/shard_map/product/pallas_call | solution.py:254
  69.6 4.4 %collective-permute-done.19.source = bf16[4,128,256]{2,1,0:T(8,128)(2,1)S(1)} collective-permute-done((bf16[4,128,256]{2,1,0:T(8,128)(2,1)S(1)}, bf16[4,128,256]{2,1,0:T(8,128)(2,1)S(1)}, u32[]{:S(2)}, u32[]{:S(2)}) %collective-permute-start.19) | collective-permute-done | bytes 262176 | tf_op jit(solution)/shard_map/ppermute | solution.py:378
  (39 shorter events, 16.7 us)
Async XLA Ops:
  0.0 2.9 %collective-permute-start.7 = (bf16[6,128,256]{2,1,0:T(8,128)(2,1)}, bf16[6,128,256]{2,1,0:T(8,128)(2,1)S(1)}, u32[]{:S(2)}, u32[]{:S(2)}) collective-permute-start(bf16[6,128,256]{2,1,0:T(8,128)(2,1)} %wave.1), channel_id=1, source_target_pairs={{0,2},{2,0},{1,3},{3,1},{4,6},{6,4},{5,7},{7,5},{8,10},{10,8},{9,1... | collective-permute-start | bytes 1179656 | tf_op jit(solution)/shard_map/ppermute | solution.py:242
  0.5 12.5 %collective-permute-start.3 = (bf16[6,128,256]{2,1,0:T(8,128)(2,1)}, bf16[6,128,256]{2,1,0:T(8,128)(2,1)S(1)}, u32[]{:S(2)}, u32[]{:S(2)}) collective-permute-start(bf16[6,128,256]{2,1,0:T(8,128)(2,1)} %wave.1), channel_id=1, source_target_pairs={{1,0},{0,1},{3,2},{2,3},{5,4},{4,5},{7,6},{6,7},{9,8},{8,9},{11,10... | collective-permute-start | bytes 1179656 | tf_op jit(solution)/shard_map/ppermute | solution.py:246
  2.9 11.8 %collective-permute-start.8 = (bf16[6,128,256]{2,1,0:T(8,128)(2,1)S(1)}, bf16[6,128,256]{2,1,0:T(8,128)(2,1)S(1)}, u32[]{:S(2)}, u32[]{:S(2)}) collective-permute-start(bf16[6,128,256]{2,1,0:T(8,128)(2,1)S(1)} %collective-permute-done.7), channel_id=1, source_target_pairs={{0,8},{2,6},{8,16},{10,2},{16,24},{18,10},{24,28},{26,18},{28,20},... | collective-permute-start | bytes 1179656 | tf_op jit(solution)/shard_map/ppermute | solution.py:239
  5.0 12.9 %collective-permute-start.1 = (bf16[6,128,256]{2,1,0:T(8,128)(2,1)}, bf16[6,128,256]{2,1,0:T(8,128)(2,1)S(1)}, u32[]{:S(2)}, u32[]{:S(2)}) collective-permute-start(bf16[6,128,256]{2,1,0:T(8,128)(2,1)} %wave.1), channel_id=1, source_target_pairs={{0,8},{2,6},{8,16},{10,2},{16,24},{18,10},{24,28},{26,18},{28,20},... | collective-permute-start | bytes 1179656 | tf_op jit(solution)/shard_map/ppermute | solution.py:239
  6.5 1.0 %copy-start = (bf16[6,128,256]{2,1,0:T(8,128)(2,1)S(1)}, bf16[6,128,256]{2,1,0:T(8,128)(2,1)}, u32[]{:S(2)}) copy-start(bf16[6,128,256]{2,1,0:T(8,128)(2,1)} %wave.1) | copy-start | bytes 1179652
  7.6 0.7 copy-start.1
  12.9 7.8 %collective-permute-start.4 = (bf16[6,128,256]{2,1,0:T(8,128)(2,1)S(1)}, bf16[6,128,256]{2,1,0:T(8,128)(2,1)S(1)}, u32[]{:S(2)}, u32[]{:S(2)}) collective-permute-start(bf16[6,128,256]{2,1,0:T(8,128)(2,1)S(1)} %collective-permute-done.3.refs_1_), channel_id=1, source_target_pairs={{0,8},{2,6},{8,16},{10,2},{16,24},{18,10},{24,28},{26,18},{28,20},... | collective-permute-start | bytes 1179656 | tf_op jit(solution)/shard_map/ppermute | solution.py:239
  14.8 10.2 %collective-permute-start.10 = (bf16[6,128,256]{2,1,0:T(8,128)(2,1)S(1)}, bf16[6,128,256]{2,1,0:T(8,128)(2,1)S(1)}, u32[]{:S(2)}, u32[]{:S(2)}) collective-permute-start(bf16[6,128,256]{2,1,0:T(8,128)(2,1)S(1)} %collective-permute-done.8.refs_4_), channel_id=1, source_target_pairs={{0,8},{2,6},{8,16},{10,2},{16,24},{18,10},{24,28},{26,18},{28,20},... | collective-permute-start | bytes 1179656 | tf_op jit(solution)/shard_map/ppermute | solution.py:239
  16.3 10.3 %collective-permute-start.9 = (bf16[6,128,256]{2,1,0:T(8,128)(2,1)S(1)}, bf16[6,128,256]{2,1,0:T(8,128)(2,1)S(1)}, u32[]{:S(2)}, u32[]{:S(2)}) collective-permute-start(bf16[6,128,256]{2,1,0:T(8,128)(2,1)S(1)} %collective-permute-done.8.refs_4_), channel_id=1, source_target_pairs={{1,0},{0,1},{3,2},{2,3},{5,4},{4,5},{7,6},{6,7},{9,8},{8,9},{11,10... | collective-permute-start | bytes 1179656 | tf_op jit(solution)/shard_map/ppermute | solution.py:246
  17.8 11.3 %collective-permute-start.2 = (bf16[6,128,256]{2,1,0:T(8,128)(2,1)S(1)}, bf16[6,128,256]{2,1,0:T(8,128)(2,1)S(1)}, u32[]{:S(2)}, u32[]{:S(2)}) collective-permute-start(bf16[6,128,256]{2,1,0:T(8,128)(2,1)S(1)} %collective-permute-done.1.refs_2_), channel_id=1, source_target_pairs={{0,8},{2,6},{8,16},{10,2},{16,24},{18,10},{24,28},{26,18},{28,20},... | collective-permute-start | bytes 1179656 | tf_op jit(solution)/shard_map/ppermute | solution.py:239
  20.7 12.6 %collective-permute-start.5 = (bf16[6,128,256]{2,1,0:T(8,128)(2,1)S(1)}, bf16[6,128,256]{2,1,0:T(8,128)(2,1)S(1)}, u32[]{:S(2)}, u32[]{:S(2)}) collective-permute-start(bf16[6,128,256]{2,1,0:T(8,128)(2,1)S(1)} %collective-permute-done.4.refs_3_), channel_id=1, source_target_pairs={{0,8},{2,6},{8,16},{10,2},{16,24},{18,10},{24,28},{26,18},{28,20},... | collective-permute-start | bytes 1179656 | tf_op jit(solution)/shard_map/ppermute | solution.py:239
  24.9 11.8 %collective-permute-start.11 = (bf16[6,128,256]{2,1,0:T(8,128)(2,1)S(1)}, bf16[6,128,256]{2,1,0:T(8,128)(2,1)S(1)}, u32[]{:S(2)}, u32[]{:S(2)}) collective-permute-start(bf16[6,128,256]{2,1,0:T(8,128)(2,1)S(1)} %collective-permute-done.10.refs_8_), channel_id=1, source_target_pairs={{1,0},{0,1},{3,2},{2,3},{5,4},{4,5},{7,6},{6,7},{9,8},{8,9},{11,10... | collective-permute-start | bytes 1179656 | tf_op jit(solution)/shard_map/ppermute | solution.py:246
  26.7 10.1 %collective-permute-start = (s32[8,128]{1,0:T(8,128)S(1)}, s32[8,128]{1,0:T(8,128)S(1)}, u32[]{:S(2)}, u32[]{:S(2)}) collective-permute-start(s32[8,128]{1,0:T(8,128)S(1)} %get-tuple-element.22.table_in), channel_id=1, source_target_pairs={{0,2},{2,0},{1,3},{3,1},{4,6},{6,4},{5,7},{7,5},{8,10},{10,8},{9,1... | collective-permute-start | bytes 12296 | tf_op jit(solution)/shard_map/ppermute | solution.py:242
  26.7 12.9 %collective-permute-start.13 = (bf16[6,128,256]{2,1,0:T(8,128)(2,1)S(1)}, bf16[6,128,256]{2,1,0:T(8,128)(2,1)S(1)}, u32[]{:S(2)}, u32[]{:S(2)}) collective-permute-start(bf16[6,128,256]{2,1,0:T(8,128)(2,1)S(1)} %collective-permute-done.10.refs_8_), channel_id=1, source_target_pairs={{0,8},{2,6},{8,16},{10,2},{16,24},{18,10},{24,28},{26,18},{28,20},... | collective-permute-start | bytes 1179656 | tf_op jit(solution)/shard_map/ppermute | solution.py:239
  33.4 8.4 %collective-permute-start.6 = (bf16[6,128,256]{2,1,0:T(8,128)(2,1)S(1)}, bf16[6,128,256]{2,1,0:T(8,128)(2,1)S(1)}, u32[]{:S(2)}, u32[]{:S(2)}) collective-permute-start(bf16[6,128,256]{2,1,0:T(8,128)(2,1)S(1)} %collective-permute-done.2.refs_6_), channel_id=1, source_target_pairs={{0,8},{2,6},{8,16},{10,2},{16,24},{18,10},{24,28},{26,18},{28,20},... | collective-permute-start | bytes 1179656 | tf_op jit(solution)/shard_map/ppermute | solution.py:239
  35.2 10.8 %collective-permute-start.12 = (bf16[6,128,256]{2,1,0:T(8,128)(2,1)S(1)}, bf16[6,128,256]{2,1,0:T(8,128)(2,1)S(1)}, u32[]{:S(2)}, u32[]{:S(2)}) collective-permute-start(bf16[6,128,256]{2,1,0:T(8,128)(2,1)S(1)} %collective-permute-done.5.refs_7_), channel_id=1, source_target_pairs={{0,8},{2,6},{8,16},{10,2},{16,24},{18,10},{24,28},{26,18},{28,20},... | collective-permute-start | bytes 1179656 | tf_op jit(solution)/shard_map/ppermute | solution.py:239
  39.5 17.1 %collective-permute-start.18 = (bf16[15,2,128,256]{3,2,1,0:T(8,128)(2,1)S(1)}, bf16[15,2,128,256]{3,2,1,0:T(8,128)(2,1)S(1)}, u32[]{:S(2)}, u32[]{:S(2)}) collective-permute-start(bf16[15,2,128,256]{3,2,1,0:T(8,128)(2,1)S(1)} %sent.3), channel_id=1, source_target_pairs={{0,2},{2,0},{1,3},{3,1},{4,6},{6,4},{5,7},{7,5},{8,10},{10,8},{9,1... | collective-permute-start | bytes 5898248 | tf_op jit(solution)/shard_map/ppermute | solution.py:242
  39.6 13.7 %collective-permute-start.14 = (bf16[6,128,256]{2,1,0:T(8,128)(2,1)S(1)}, bf16[6,128,256]{2,1,0:T(8,128)(2,1)S(1)}, u32[]{:S(2)}, u32[]{:S(2)}) collective-permute-start(bf16[6,128,256]{2,1,0:T(8,128)(2,1)S(1)} %collective-permute-done.13.refs_2_.refs_0_), channel_id=1, source_target_pairs={{1,0},{0,1},{3,2},{2,3},{5,4},{4,5},{7,6},{6,7},{9,8},{8,9},{11,10... | collective-permute-start | bytes 1179656 | tf_op jit(solution)/shard_map/ppermute | solution.py:246
  41.8 11.5 %collective-permute-start.15 = (bf16[6,128,256]{2,1,0:T(8,128)(2,1)S(1)}, bf16[6,128,256]{2,1,0:T(8,128)(2,1)S(1)}, u32[]{:S(2)}, u32[]{:S(2)}) collective-permute-start(bf16[6,128,256]{2,1,0:T(8,128)(2,1)S(1)} %collective-permute-done.6.refs_10_.refs_0_), channel_id=1, source_target_pairs={{0,8},{2,6},{8,16},{10,2},{16,24},{18,10},{24,28},{26,18},{28,20},... | collective-permute-start | bytes 1179656 | tf_op jit(solution)/shard_map/ppermute | solution.py:239
  46.0 8.4 %collective-permute-start.16 = (bf16[6,128,256]{2,1,0:T(8,128)(2,1)S(1)}, bf16[6,128,256]{2,1,0:T(8,128)(2,1)S(1)}, u32[]{:S(2)}, u32[]{:S(2)}) collective-permute-start(bf16[6,128,256]{2,1,0:T(8,128)(2,1)S(1)} %collective-permute-done.12.refs_11_.refs_1_), channel_id=1, source_target_pairs={{0,8},{2,6},{8,16},{10,2},{16,24},{18,10},{24,28},{26,18},{28,20},... | collective-permute-start | bytes 1179656 | tf_op jit(solution)/shard_map/ppermute | solution.py:239
  56.5 3.5 %collective-permute-start.17 = (bf16[9,2,128,256]{3,2,1,0:T(8,128)(2,1)S(1)}, bf16[9,2,128,256]{3,2,1,0:T(8,128)(2,1)S(1)}, u32[]{:S(2)}, u32[]{:S(2)}) collective-permute-start(bf16[9,2,128,256]{3,2,1,0:T(8,128)(2,1)S(1)} %sent.2), channel_id=1, source_target_pairs={{0,2},{2,0},{1,3},{3,1},{4,6},{6,4},{5,7},{7,5},{8,10},{10,8},{9,1... | collective-permute-start | bytes 3538952 | tf_op jit(solution)/shard_map/ppermute | solution.py:242
  64.9 9.1 %collective-permute-start.19 = (bf16[4,128,256]{2,1,0:T(8,128)(2,1)S(1)}, bf16[4,128,256]{2,1,0:T(8,128)(2,1)S(1)}, u32[]{:S(2)}, u32[]{:S(2)}) collective-permute-start(bf16[4,128,256]{2,1,0:T(8,128)(2,1)S(1)} %bitcast.2), channel_id=1, source_target_pairs={{0,1},{1,0},{2,3},{3,2},{4,5},{5,4},{6,7},{7,6},{8,9},{9,8},{10,11... | collective-permute-start | bytes 786440 | tf_op jit(solution)/shard_map/ppermute | solution.py:378
  69.3 7.5 %collective-permute-start.20 = (bf16[2,128,256]{2,1,0:T(8,128)(2,1)S(1)}, bf16[2,128,256]{2,1,0:T(8,128)(2,1)S(1)}, u32[]{:S(2)}, u32[]{:S(2)}) collective-permute-start(bf16[2,128,256]{2,1,0:T(8,128)(2,1)S(1)} %bitcast.3), channel_id=1, source_target_pairs={{0,1},{1,0},{2,3},{3,2},{4,5},{5,4},{6,7},{7,6},{8,9},{9,8},{10,11... | collective-permute-start | bytes 393224 | tf_op jit(solution)/shard_map/ppermute | solution.py:378
  74.1 0.7 copy-start.4
  (2 other events, 1.3 us)

commit v2 on v0

--- a/solution.py
+++ b/solution.py
@@ -9,7 +9,7 @@
 
 ORDER, START, SECTOR, CLASS, LATER = range(5)
 TABLE = (8, 128)
-LIMITS = dict(table=4, sent=8, load=32, fill=8, product=24)
+LIMITS = dict(table=4, sent=12, load=32, fill=16, product=28)
 
 
 def ring_position(chip, chips):
@@ -17,7 +17,7 @@
 
 
 def table_kernel(sizes, early, owner_map, local_map, op_class, wave, *refs):
-    targets, terms, classes, op_size, chips = sizes
+    targets, terms, classes, op_size, chips, _ = sizes
     half = chips // 2
     core = lax.axis_index("core")
     place = ring_position(lax.axis_index("chip"), chips)
@@ -75,11 +75,15 @@
     wave_copy.wait()
 
 
-def fetch(unit, sector, target, sem):
+def fetch(near, unit, sector, target, r, sem):
     op_size = len(unit)
     me = lax.axis_index("op")
     for j, source in enumerate(unit):
-        pltpu.make_async_copy(source.at[sector], target.at[lax.rem(me + j, op_size)], sem).start()
+        turn = lax.rem(me + j, op_size)
+        if near:
+            target[r, turn] = source[sector]
+        else:
+            pltpu.make_async_copy(source.at[sector], target.at[r, turn], sem).start()
 
 
 def read_table(source, target, sem):
@@ -93,7 +97,7 @@
 
 
 def sent_kernel(sizes, low, high, asked_in, *refs):
-    chips, op_size = sizes[4], sizes[3]
+    op_size, chips, near = sizes[3:]
     *units, sent, table, slot_sems, sem = refs
     read_table(asked_in, table, sem)
     skipped = table[START, chips + low]
@@ -102,32 +106,41 @@
         @pl.loop(table[START, chips + u], table[START, chips + u + 1])
         def _(i):
             slot = i - skipped
-            fetch(unit, table[SECTOR, table[ORDER, i]], sent.at[slot], slot_sems.at[slot])
+            fetch(near, unit, table[SECTOR, table[ORDER, i]], sent, slot, slot_sems.at[slot])
+
+    if near:
+        return
 
     @pl.loop(0, table[START, chips + high] - skipped)
     def _(slot):
         pltpu.make_async_copy(sent.at[slot], sent.at[slot], slot_sems.at[slot]).wait()
 
 
-def fetch_own(units, low, table, blocks, block_sems):
+def fetch_own(near, units, low, table, blocks, block_sems):
     for u, unit in enumerate(units, low):
 
         @pl.loop(table[START, u], table[START, u + 1])
         def _(i):
             r = table[ORDER, i]
-            fetch(unit, table[SECTOR, r], blocks.at[r], block_sems.at[r])
-
-
-def fetch_received(received, first, last, table, blocks, block_sems):
+            fetch(near, unit, table[SECTOR, r], blocks, r, block_sems.at[r])
+
+
+def fetch_received(near, received, first, last, table, blocks, block_sems):
     skipped = table[START, first]
 
     @pl.loop(skipped, table[START, last])
     def _(i):
         r = table[ORDER, i]
-        pltpu.make_async_copy(received.at[i - skipped], blocks.at[r], block_sems.at[r]).start()
-
-
-def wait_blocks(first, last, table, blocks, block_sems):
+        if near:
+            blocks[r] = received[i - skipped]
+        else:
+            pltpu.make_async_copy(received.at[i - skipped], blocks.at[r], block_sems.at[r]).start()
+
+
+def wait_blocks(near, first, last, table, blocks, block_sems):
+    if near:
+        return
+
     @pl.loop(table[START, first], table[START, last])
     def _(i):
         r = table[ORDER, i]
@@ -143,8 +156,8 @@
     for load in loads:
         load.start()
     read_table(table_in, table, sems.at[2])
-    fetch_own(grouped(units, sizes[3]), 0, table, blocks, block_sems)
-    wait_blocks(0, early, table, blocks, block_sems)
+    fetch_own(sizes[5], grouped(units, sizes[3]), 0, table, blocks, block_sems)
+    wait_blocks(sizes[5], 0, early, table, blocks, block_sems)
     for load in loads:
         load.wait()
 
@@ -153,28 +166,28 @@
     chips = sizes[4]
     *units, _, blocks, table, block_sems, sem = refs
     read_table(table_in, table, sem)
-    fetch_received(received, chips, chips + early, table, blocks, block_sems)
-    fetch_own(grouped(units, sizes[3]), early, table, blocks, block_sems)
-    wait_blocks(early, chips + early, table, blocks, block_sems)
+    fetch_received(sizes[5], received, chips, chips + early, table, blocks, block_sems)
+    fetch_own(sizes[5], grouped(units, sizes[3]), early, table, blocks, block_sems)
+    wait_blocks(sizes[5], early, chips + early, table, blocks, block_sems)
 
 
 def product_kernel(sizes, early, first, count, table_in, received, lefts, rights, _, *refs):
-    targets, terms, classes, op_size, chips = sizes
+    targets, terms, classes, op_size, chips, near = sizes
     keep, send, blocks, table, block_sems, sem = refs
     size = lefts.shape[-1]
     rows = size // op_size
     me = lax.axis_index("op")
     read_table(table_in, table, sem)
     if first == 0:
-        fetch_received(received, chips + early, 2 * chips, table, blocks, block_sems)
+        fetch_received(near, received, chips + early, 2 * chips, table, blocks, block_sems)
         if count < targets:
-            wait_blocks(chips + early, 2 * chips, table, blocks, block_sems)
+            wait_blocks(near, chips + early, 2 * chips, table, blocks, block_sems)
 
     @pl.loop(0, count)
     def _(step):
         t = first + step
 
-        if count == targets:
+        if count == targets and not near:
 
             @pl.loop(0, classes)
             def _(c):
@@ -220,7 +233,8 @@
     classes = owner_map.shape[1]
     half = chips // 2
     asked = targets * classes
-    sizes = (targets, terms, classes, op_size, chips)
+    near = chips * op_size * wave.size <= 4 * 1024 * 1024
+    sizes = (targets, terms, classes, op_size, chips, near)
     early = chips - 3
     most = max(2, (asked + 2 * chips - 1) // (2 * chips) + 1)
     ring = list(range(0, chips, 2)) + list(range(1, chips, 2))[::-1]
@@ -245,11 +259,12 @@
     whole = pl.BlockSpec(memory_space=pltpu.VMEM)
     scalars = pl.BlockSpec(memory_space=pltpu.SMEM)
     apart = pl.BlockSpec(memory_space=pl.ANY)
+    held_in = whole if near else apart
     def call(kernel, name, operands, outs, scratch, specs=None, aliases={}, flops=0):
         return pl.pallas_call(
             kernel,
             name=name,
-            in_specs=specs or [whole] + [apart] * (len(operands) - 1),
+            in_specs=specs or [whole] + [held_in] * (len(operands) - 1),
             out_specs=[whole] * len(outs),
             out_shape=outs,
             input_output_aliases=aliases,
@@ -328,6 +343,7 @@
         [table, left_ops, right_ops] + flat(0, early, ()),
         operators_out + [blocks_out],
         [pltpu.SemaphoreType.DMA((asked,)), pltpu.SemaphoreType.DMA((3,))],
+        [whole] + [apart] * 2 + [held_in] * (early * op_size),
     )
     late = flat(early, chips)
     received = gather(early, chips, [lax.optimization_barrier((late[0], lefts))[0]] + late[1:])
@@ -338,7 +354,7 @@
         operands,
         [blocks_out],
         block_sems,
-        [whole] + [apart] * (len(late) + 1) + [whole],
+        [whole] + [held_in] * (len(late) + 1) + [whole],
         {len(operands) - 1: 0},
     )
 
@@ -355,7 +371,7 @@
                 blocks_out,
             ],
             block_sems,
-            [whole, apart] + [whole] * 3,
+            [whole, held_in] + [whole] * 3,
             {4: 2},
             4 * count * terms * size**3,
         )

time: 78.2 us -> 74.9 us (0.958)
  Pallas kernels: 23.8 us -> 17.6 us
  waiting for transfers between devices: 19.3 us -> 22.7 us
    pallas_call x7, Pallas kernels: 23.8 us -> 17.6 us  [call(): pl.pallas_call(kernel, name=name, in_specs=specs or [whole] + [held_in] *...]
    ppermute x4, waiting for transfers between devices: 0.01 us -> 1.64 us  [swap(): return lax.ppermute(x, 'core', [(0, 1), (1, 0)])]
    ppermute x11, waiting for transfers between devices: 13.7 us -> 15.3 us  [hop(): return lax.ppermute(x, ('chip', 'core'), pairs)]
  transfers between devices with their start and end apart: 21 -> 21, of which waited for: 10 -> 11; matrix products, arithmetic and copies ran while one was open for 1% -> 2% of each run, Pallas kernels for 24% -> 18%
where the time goes in v2:
time: 74.9 us; the launch traced here: 74.6 us
  starting transfers between devices  29.1 us (39%)
  waiting for transfers between devices  22.7 us (30%)
  Pallas kernels  17.6 us (23%)
  local copies, waits for them, and re-layouts  3.06 us (4%)
  other arithmetic  1.98 us (3%)
    ppermute x11, starting transfers between devices, hop(): return lax.ppermute(x, ('chip', 'core'), pairs)  19 us
    pallas_call x7, Pallas kernels, call(): pl.pallas_call(kernel, name=name, in_specs=specs or [whole] + [held_in] *...  17.6 us
    ppermute x11, waiting for transfers between devices, hop(): return lax.ppermute(x, ('chip', 'core'), pairs)  15.3 us
    ppermute x4, starting transfers between devices, across(): lax.ppermute(x, 'op', [((q + j) % op_size, q) for q in range(op_size)])  7.28 us
    ppermute x2, waiting for transfers between devices, shards(): part = lax.ppermute(send[k - 1], 'op', turn)  5.35 us
    unnamed x10, local copies, waits for them, and re-layouts  3.06 us
    ppermute x2, starting transfers between devices, shards(): part = lax.ppermute(send[k - 1], 'op', turn)  2.17 us
    ppermute x4, waiting for transfers between devices, swap(): return lax.ppermute(x, 'core', [(0, 1), (1, 0)])  1.64 us
  transfers between devices with their start and end apart: 21, of which 11 were waited for; matrix products, arithmetic and copies ran while one was open for 2% of the time, Pallas kernels for 18%

profile of v2, /device:TPU:0, one launch (start us, length us, event | category | flops | bytes accessed | tf_op | source)
XLA Modules:
  0.0 74.6 jit_solution(10393040881698328187)
XLA Ops:
  0.5 2.5 %collective-permute-start.3 = (bf16[6,128,256]{2,1,0:T(8,128)(2,1)}, bf16[6,128,256]{2,1,0:T(8,128)(2,1)S(1)}, u32[]{:S(2)}, u32[]{:S(2)}) collective-permute-start(bf16[6,128,256]{2,1,0:T(8,128)(2,1)} %wave.1), channel_id=1, source_target_pairs={{1,0},{0,1},{3,2},{2,3},{5,4},{4,5},{7,6},{6,7},{9,8},{8,9},{11,10... | collective-permute-start | bytes 1179656 | tf_op jit(solution)/shard_map/ppermute | solution.py:255
  2.9 2.0 %collective-permute-start.8 = (bf16[6,128,256]{2,1,0:T(8,128)(2,1)S(1)}, bf16[6,128,256]{2,1,0:T(8,128)(2,1)S(1)}, u32[]{:S(2)}, u32[]{:S(2)}) collective-permute-start(bf16[6,128,256]{2,1,0:T(8,128)(2,1)S(1)} %collective-permute-done.7), channel_id=1, source_target_pairs={{0,8},{2,6},{8,16},{10,2},{16,24},{18,10},{24,28},{26,18},{28,20},... | collective-permute-start | bytes 1179656 | tf_op jit(solution)/shard_map/ppermute | solution.py:248
  5.0 1.6 %collective-permute-start.1 = (bf16[6,128,256]{2,1,0:T(8,128)(2,1)}, bf16[6,128,256]{2,1,0:T(8,128)(2,1)S(1)}, u32[]{:S(2)}, u32[]{:S(2)}) collective-permute-start(bf16[6,128,256]{2,1,0:T(8,128)(2,1)} %wave.1), channel_id=1, source_target_pairs={{0,8},{2,6},{8,16},{10,2},{16,24},{18,10},{24,28},{26,18},{28,20},... | collective-permute-start | bytes 1179656 | tf_op jit(solution)/shard_map/ppermute | solution.py:248
  9.6 2.9 %table.1 = (s32[8,128]{1,0:T(8,128)S(1)}, bf16[6,128,256]{2,1,0:T(8,128)(2,1)S(1)}) custom-call(s32[6,5]{1,0:T(8,128)S(1)} %copy-done.2, s32[6,5]{1,0:T(8,128)S(1)} %copy-done.3, s32[8]{0:T(128)S(1)} %copy-done.4, bf16[6,128,256]{2,1,0:T(8,128)(2,1)S(1)} %copy-done.1), custom_call_target="tpu_custom_call" | custom-call | bytes 395264 | tf_op jit(solution)/shard_map/table/pallas_call | solution.py:264
  12.9 1.8 %collective-permute-start.4 = (bf16[6,128,256]{2,1,0:T(8,128)(2,1)S(1)}, bf16[6,128,256]{2,1,0:T(8,128)(2,1)S(1)}, u32[]{:S(2)}, u32[]{:S(2)}) collective-permute-start(bf16[6,128,256]{2,1,0:T(8,128)(2,1)S(1)} %collective-permute-done.3.refs_1_), channel_id=1, source_target_pairs={{0,8},{2,6},{8,16},{10,2},{16,24},{18,10},{24,28},{26,18},{28,20},... | collective-permute-start | bytes 1179656 | tf_op jit(solution)/shard_map/ppermute | solution.py:248
  14.8 1.6 %collective-permute-start.10 = (bf16[6,128,256]{2,1,0:T(8,128)(2,1)S(1)}, bf16[6,128,256]{2,1,0:T(8,128)(2,1)S(1)}, u32[]{:S(2)}, u32[]{:S(2)}) collective-permute-start(bf16[6,128,256]{2,1,0:T(8,128)(2,1)S(1)} %collective-permute-done.8.refs_4_), channel_id=1, source_target_pairs={{0,8},{2,6},{8,16},{10,2},{16,24},{18,10},{24,28},{26,18},{28,20},... | collective-permute-start | bytes 1179656 | tf_op jit(solution)/shard_map/ppermute | solution.py:248
  17.8 1.6 %collective-permute-start.2 = (bf16[6,128,256]{2,1,0:T(8,128)(2,1)S(1)}, bf16[6,128,256]{2,1,0:T(8,128)(2,1)S(1)}, u32[]{:S(2)}, u32[]{:S(2)}) collective-permute-start(bf16[6,128,256]{2,1,0:T(8,128)(2,1)S(1)} %collective-permute-done.1.refs_2_), channel_id=1, source_target_pairs={{0,8},{2,6},{8,16},{10,2},{16,24},{18,10},{24,28},{26,18},{28,20},... | collective-permute-start | bytes 1179656 | tf_op jit(solution)/shard_map/ppermute | solution.py:248
  20.7 1.8 %collective-permute-start.5 = (bf16[6,128,256]{2,1,0:T(8,128)(2,1)S(1)}, bf16[6,128,256]{2,1,0:T(8,128)(2,1)S(1)}, u32[]{:S(2)}, u32[]{:S(2)}) collective-permute-start(bf16[6,128,256]{2,1,0:T(8,128)(2,1)S(1)} %collective-permute-done.4.refs_3_), channel_id=1, source_target_pairs={{0,8},{2,6},{8,16},{10,2},{16,24},{18,10},{24,28},{26,18},{28,20},... | collective-permute-start | bytes 1179656 | tf_op jit(solution)/shard_map/ppermute | solution.py:248
  22.5 2.4 %collective-permute-done.10.refs_8_ = bf16[6,128,256]{2,1,0:T(8,128)(2,1)S(1)} collective-permute-done((bf16[6,128,256]{2,1,0:T(8,128)(2,1)S(1)}, bf16[6,128,256]{2,1,0:T(8,128)(2,1)S(1)}, u32[]{:S(2)}, u32[]{:S(2)}) %collective-permute-start.10) | collective-permute-done | bytes 393248 | tf_op jit(solution)/shard_map/ppermute | solution.py:248
  24.9 1.7 %collective-permute-start.11 = (bf16[6,128,256]{2,1,0:T(8,128)(2,1)S(1)}, bf16[6,128,256]{2,1,0:T(8,128)(2,1)S(1)}, u32[]{:S(2)}, u32[]{:S(2)}) collective-permute-start(bf16[6,128,256]{2,1,0:T(8,128)(2,1)S(1)} %collective-permute-done.10.refs_8_), channel_id=1, source_target_pairs={{1,0},{0,1},{3,2},{2,3},{5,4},{4,5},{7,6},{6,7},{9,8},{8,9},{11,10... | collective-permute-start | bytes 1179656 | tf_op jit(solution)/shard_map/ppermute | solution.py:255
  26.7 1.6 %collective-permute-start.13 = (bf16[6,128,256]{2,1,0:T(8,128)(2,1)S(1)}, bf16[6,128,256]{2,1,0:T(8,128)(2,1)S(1)}, u32[]{:S(2)}, u32[]{:S(2)}) collective-permute-start(bf16[6,128,256]{2,1,0:T(8,128)(2,1)S(1)} %collective-permute-done.10.refs_8_), channel_id=1, source_target_pairs={{0,8},{2,6},{8,16},{10,2},{16,24},{18,10},{24,28},{26,18},{28,20},... | collective-permute-start | bytes 1179656 | tf_op jit(solution)/shard_map/ppermute | solution.py:248
  29.1 4.2 %collective-permute-done.5.refs_7_ = bf16[6,128,256]{2,1,0:T(8,128)(2,1)S(1)} collective-permute-done((bf16[6,128,256]{2,1,0:T(8,128)(2,1)S(1)}, bf16[6,128,256]{2,1,0:T(8,128)(2,1)S(1)}, u32[]{:S(2)}, u32[]{:S(2)}) %collective-permute-start.5) | collective-permute-done | bytes 393248 | tf_op jit(solution)/shard_map/ppermute | solution.py:248
  33.4 1.8 %collective-permute-start.6 = (bf16[6,128,256]{2,1,0:T(8,128)(2,1)S(1)}, bf16[6,128,256]{2,1,0:T(8,128)(2,1)S(1)}, u32[]{:S(2)}, u32[]{:S(2)}) collective-permute-start(bf16[6,128,256]{2,1,0:T(8,128)(2,1)S(1)} %collective-permute-done.2.refs_6_), channel_id=1, source_target_pairs={{0,8},{2,6},{8,16},{10,2},{16,24},{18,10},{24,28},{26,18},{28,20},... | collective-permute-start | bytes 1179656 | tf_op jit(solution)/shard_map/ppermute | solution.py:248
  39.4 2.4 %collective-permute-done.6.refs_0_ = bf16[6,128,256]{2,1,0:T(8,128)(2,1)S(1)} collective-permute-done((bf16[6,128,256]{2,1,0:T(8,128)(2,1)S(1)}, bf16[6,128,256]{2,1,0:T(8,128)(2,1)S(1)}, u32[]{:S(2)}, u32[]{:S(2)}) %collective-permute-start.6) | collective-permute-done | bytes 393248 | tf_op jit(solution)/shard_map/ppermute | solution.py:248
  41.8 1.8 %collective-permute-start.15 = (bf16[6,128,256]{2,1,0:T(8,128)(2,1)S(1)}, bf16[6,128,256]{2,1,0:T(8,128)(2,1)S(1)}, u32[]{:S(2)}, u32[]{:S(2)}) collective-permute-start(bf16[6,128,256]{2,1,0:T(8,128)(2,1)S(1)} %collective-permute-done.6.refs_0_), channel_id=1, source_target_pairs={{0,8},{2,6},{8,16},{10,2},{16,24},{18,10},{24,28},{26,18},{28,20},... | collective-permute-start | bytes 1179656 | tf_op jit(solution)/shard_map/ppermute | solution.py:248
  43.6 2.4 %collective-permute-done.12.refs_1_ = bf16[6,128,256]{2,1,0:T(8,128)(2,1)S(1)} collective-permute-done((bf16[6,128,256]{2,1,0:T(8,128)(2,1)S(1)}, bf16[6,128,256]{2,1,0:T(8,128)(2,1)S(1)}, u32[]{:S(2)}, u32[]{:S(2)}) %collective-permute-start.12) | collective-permute-done | bytes 393248 | tf_op jit(solution)/shard_map/ppermute | solution.py:248
  46.0 1.8 %collective-permute-start.16 = (bf16[6,128,256]{2,1,0:T(8,128)(2,1)S(1)}, bf16[6,128,256]{2,1,0:T(8,128)(2,1)S(1)}, u32[]{:S(2)}, u32[]{:S(2)}) collective-permute-start(bf16[6,128,256]{2,1,0:T(8,128)(2,1)S(1)} %collective-permute-done.12.refs_1_), channel_id=1, source_target_pairs={{0,8},{2,6},{8,16},{10,2},{16,24},{18,10},{24,28},{26,18},{28,20},... | collective-permute-start | bytes 1179656 | tf_op jit(solution)/shard_map/ppermute | solution.py:248
  47.8 4.9 %load.1 = (bf16[6,8,256,256]{3,2,1,0:T(8,128)(2,1)S(1)}, bf16[6,8,256,256]{3,2,1,0:T(8,128)(2,1)S(1)}, bf16[30,2,128,256]{3,2,1,0:T(8,128)(2,1)S(1)}) custom-call(s32[8,128]{1,0:T(8,128)S(1)} %get-tuple-element.22.table_in, bf16[6,8,256,256]{3,2,1,0:T(8,128)(2,1)} %left.1, bf16[6,8,256,256]{3,2,1,0:T(8,128)(2,1)} %right.1, ...), custom_call_target="tpu_custom_call" | custom-call | bytes 16515072 | tf_op jit(solution)/shard_map/load/pallas_call | solution.py:264
  52.8 1.7 %collective-permute-done.16.refs_5_ = bf16[6,128,256]{2,1,0:T(8,128)(2,1)S(1)} collective-permute-done((bf16[6,128,256]{2,1,0:T(8,128)(2,1)S(1)}, bf16[6,128,256]{2,1,0:T(8,128)(2,1)S(1)}, u32[]{:S(2)}, u32[]{:S(2)}) %collective-permute-start.16) | collective-permute-done | bytes 393248 | tf_op jit(solution)/shard_map/ppermute | solution.py:248
  56.5 1.6 %collective-permute-done.17.received = bf16[9,2,128,256]{3,2,1,0:T(8,128)(2,1)S(1)} collective-permute-done((bf16[9,2,128,256]{3,2,1,0:T(8,128)(2,1)S(1)}, bf16[9,2,128,256]{3,2,1,0:T(8,128)(2,1)S(1)}, u32[]{:S(2)}, u32[]{:S(2)}) %collective-permute-start.17) | collective-permute-done | bytes 1179680 | tf_op jit(solution)/shard_map/ppermute | solution.py:251
  58.2 4.3 %product.2 = (f32[4,128,256]{2,1,0:T(8,128)S(1)}, bf16[1,4,128,256]{3,2,1,0:T(8,128)(2,1)S(1)}, bf16[30,2,128,256]{3,2,1,0:T(8,128)(2,1)S(1)}) custom-call(s32[8,128]{1,0:T(8,128)S(1)} %get-tuple-element.22.table_in, bf16[9,2,128,256]{3,2,1,0:T(8,128)(2,1)S(1)} %collective-permute-done.17.received, ...), custom_call_target="tpu_custom_call", output_to_operand_aliasing={{2}: (4, {})} | custom-call | flops 2147483648 | bytes 4456448 | tf_op jit(solution)/shard_map/product/pallas_call | solution.py:264
  62.5 1.8 %collective-permute-start.19 = (bf16[4,128,256]{2,1,0:T(8,128)(2,1)S(1)}, bf16[4,128,256]{2,1,0:T(8,128)(2,1)}, u32[]{:S(2)}, u32[]{:S(2)}) collective-permute-start(bf16[4,128,256]{2,1,0:T(8,128)(2,1)S(1)} %bitcast.2), channel_id=1, source_target_pairs={{0,1},{1,0},{2,3},{3,2},{4,5},{5,4},{6,7},{7,6},{8,9},{9,8},{10,11... | collective-permute-start | bytes 786440 | tf_op jit(solution)/shard_map/ppermute | solution.py:380
  64.3 2.6 %product.3 = (f32[2,128,256]{2,1,0:T(8,128)S(1)}, bf16[1,2,128,256]{3,2,1,0:T(8,128)(2,1)S(1)}, bf16[30,2,128,256]{3,2,1,0:T(8,128)(2,1)S(1)}) custom-call(s32[8,128]{1,0:T(8,128)S(1)} %get-tuple-element.22.table_in, bf16[9,2,128,256]{3,2,1,0:T(8,128)(2,1)S(1)} %collective-permute-done.17.received, ...), custom_call_target="tpu_custom_call", output_to_operand_aliasing={{2}: (4, {})} | custom-call | flops 1073741824 | bytes 4194304 | tf_op jit(solution)/shard_map/product/pallas_call | solution.py:264
  67.3 4.6 %collective-permute-done.19.source = bf16[4,128,256]{2,1,0:T(8,128)(2,1)} collective-permute-done((bf16[4,128,256]{2,1,0:T(8,128)(2,1)S(1)}, bf16[4,128,256]{2,1,0:T(8,128)(2,1)}, u32[]{:S(2)}, u32[]{:S(2)}) %collective-permute-start.19) | collective-permute-done | bytes 262176 | tf_op jit(solution)/shard_map/ppermute | solution.py:380
  (39 shorter events, 17.0 us)
Async XLA Ops:
  0.0 2.9 %collective-permute-start.7 = (bf16[6,128,256]{2,1,0:T(8,128)(2,1)}, bf16[6,128,256]{2,1,0:T(8,128)(2,1)S(1)}, u32[]{:S(2)}, u32[]{:S(2)}) collective-permute-start(bf16[6,128,256]{2,1,0:T(8,128)(2,1)} %wave.1), channel_id=1, source_target_pairs={{0,2},{2,0},{1,3},{3,1},{4,6},{6,4},{5,7},{7,5},{8,10},{10,8},{9,1... | collective-permute-start | bytes 1179656 | tf_op jit(solution)/shard_map/ppermute | solution.py:251
  0.5 12.5 %collective-permute-start.3 = (bf16[6,128,256]{2,1,0:T(8,128)(2,1)}, bf16[6,128,256]{2,1,0:T(8,128)(2,1)S(1)}, u32[]{:S(2)}, u32[]{:S(2)}) collective-permute-start(bf16[6,128,256]{2,1,0:T(8,128)(2,1)} %wave.1), channel_id=1, source_target_pairs={{1,0},{0,1},{3,2},{2,3},{5,4},{4,5},{7,6},{6,7},{9,8},{8,9},{11,10... | collective-permute-start | bytes 1179656 | tf_op jit(solution)/shard_map/ppermute | solution.py:255
  2.9 11.8 %collective-permute-start.8 = (bf16[6,128,256]{2,1,0:T(8,128)(2,1)S(1)}, bf16[6,128,256]{2,1,0:T(8,128)(2,1)S(1)}, u32[]{:S(2)}, u32[]{:S(2)}) collective-permute-start(bf16[6,128,256]{2,1,0:T(8,128)(2,1)S(1)} %collective-permute-done.7), channel_id=1, source_target_pairs={{0,8},{2,6},{8,16},{10,2},{16,24},{18,10},{24,28},{26,18},{28,20},... | collective-permute-start | bytes 1179656 | tf_op jit(solution)/shard_map/ppermute | solution.py:248
  5.0 12.9 %collective-permute-start.1 = (bf16[6,128,256]{2,1,0:T(8,128)(2,1)}, bf16[6,128,256]{2,1,0:T(8,128)(2,1)S(1)}, u32[]{:S(2)}, u32[]{:S(2)}) collective-permute-start(bf16[6,128,256]{2,1,0:T(8,128)(2,1)} %wave.1), channel_id=1, source_target_pairs={{0,8},{2,6},{8,16},{10,2},{16,24},{18,10},{24,28},{26,18},{28,20},... | collective-permute-start | bytes 1179656 | tf_op jit(solution)/shard_map/ppermute | solution.py:248
  6.5 1.0 %copy-start.1 = (bf16[6,128,256]{2,1,0:T(8,128)(2,1)S(1)}, bf16[6,128,256]{2,1,0:T(8,128)(2,1)}, u32[]{:S(2)}) copy-start(bf16[6,128,256]{2,1,0:T(8,128)(2,1)} %wave.1) | copy-start | bytes 1179652
  7.6 0.7 copy-start.2
  12.9 7.8 %collective-permute-start.4 = (bf16[6,128,256]{2,1,0:T(8,128)(2,1)S(1)}, bf16[6,128,256]{2,1,0:T(8,128)(2,1)S(1)}, u32[]{:S(2)}, u32[]{:S(2)}) collective-permute-start(bf16[6,128,256]{2,1,0:T(8,128)(2,1)S(1)} %collective-permute-done.3.refs_1_), channel_id=1, source_target_pairs={{0,8},{2,6},{8,16},{10,2},{16,24},{18,10},{24,28},{26,18},{28,20},... | collective-permute-start | bytes 1179656 | tf_op jit(solution)/shard_map/ppermute | solution.py:248
  14.8 10.2 %collective-permute-start.10 = (bf16[6,128,256]{2,1,0:T(8,128)(2,1)S(1)}, bf16[6,128,256]{2,1,0:T(8,128)(2,1)S(1)}, u32[]{:S(2)}, u32[]{:S(2)}) collective-permute-start(bf16[6,128,256]{2,1,0:T(8,128)(2,1)S(1)} %collective-permute-done.8.refs_4_), channel_id=1, source_target_pairs={{0,8},{2,6},{8,16},{10,2},{16,24},{18,10},{24,28},{26,18},{28,20},... | collective-permute-start | bytes 1179656 | tf_op jit(solution)/shard_map/ppermute | solution.py:248
  16.3 10.3 %collective-permute-start.9 = (bf16[6,128,256]{2,1,0:T(8,128)(2,1)S(1)}, bf16[6,128,256]{2,1,0:T(8,128)(2,1)S(1)}, u32[]{:S(2)}, u32[]{:S(2)}) collective-permute-start(bf16[6,128,256]{2,1,0:T(8,128)(2,1)S(1)} %collective-permute-done.8.refs_4_), channel_id=1, source_target_pairs={{1,0},{0,1},{3,2},{2,3},{5,4},{4,5},{7,6},{6,7},{9,8},{8,9},{11,10... | collective-permute-start | bytes 1179656 | tf_op jit(solution)/shard_map/ppermute | solution.py:255
  17.8 11.3 %collective-permute-start.2 = (bf16[6,128,256]{2,1,0:T(8,128)(2,1)S(1)}, bf16[6,128,256]{2,1,0:T(8,128)(2,1)S(1)}, u32[]{:S(2)}, u32[]{:S(2)}) collective-permute-start(bf16[6,128,256]{2,1,0:T(8,128)(2,1)S(1)} %collective-permute-done.1.refs_2_), channel_id=1, source_target_pairs={{0,8},{2,6},{8,16},{10,2},{16,24},{18,10},{24,28},{26,18},{28,20},... | collective-permute-start | bytes 1179656 | tf_op jit(solution)/shard_map/ppermute | solution.py:248
  20.7 12.6 %collective-permute-start.5 = (bf16[6,128,256]{2,1,0:T(8,128)(2,1)S(1)}, bf16[6,128,256]{2,1,0:T(8,128)(2,1)S(1)}, u32[]{:S(2)}, u32[]{:S(2)}) collective-permute-start(bf16[6,128,256]{2,1,0:T(8,128)(2,1)S(1)} %collective-permute-done.4.refs_3_), channel_id=1, source_target_pairs={{0,8},{2,6},{8,16},{10,2},{16,24},{18,10},{24,28},{26,18},{28,20},... | collective-permute-start | bytes 1179656 | tf_op jit(solution)/shard_map/ppermute | solution.py:248
  24.9 11.8 %collective-permute-start.11 = (bf16[6,128,256]{2,1,0:T(8,128)(2,1)S(1)}, bf16[6,128,256]{2,1,0:T(8,128)(2,1)S(1)}, u32[]{:S(2)}, u32[]{:S(2)}) collective-permute-start(bf16[6,128,256]{2,1,0:T(8,128)(2,1)S(1)} %collective-permute-done.10.refs_8_), channel_id=1, source_target_pairs={{1,0},{0,1},{3,2},{2,3},{5,4},{4,5},{7,6},{6,7},{9,8},{8,9},{11,10... | collective-permute-start | bytes 1179656 | tf_op jit(solution)/shard_map/ppermute | solution.py:255
  26.7 10.1 %collective-permute-start = (s32[8,128]{1,0:T(8,128)S(1)}, s32[8,128]{1,0:T(8,128)S(1)}, u32[]{:S(2)}, u32[]{:S(2)}) collective-permute-start(s32[8,128]{1,0:T(8,128)S(1)} %get-tuple-element.22.table_in), channel_id=1, source_target_pairs={{0,2},{2,0},{1,3},{3,1},{4,6},{6,4},{5,7},{7,5},{8,10},{10,8},{9,1... | collective-permute-start | bytes 12296 | tf_op jit(solution)/shard_map/ppermute | solution.py:251
  26.7 11.1 %collective-permute-start.13 = (bf16[6,128,256]{2,1,0:T(8,128)(2,1)S(1)}, bf16[6,128,256]{2,1,0:T(8,128)(2,1)S(1)}, u32[]{:S(2)}, u32[]{:S(2)}) collective-permute-start(bf16[6,128,256]{2,1,0:T(8,128)(2,1)S(1)} %collective-permute-done.10.refs_8_), channel_id=1, source_target_pairs={{0,8},{2,6},{8,16},{10,2},{16,24},{18,10},{24,28},{26,18},{28,20},... | collective-permute-start | bytes 1179656 | tf_op jit(solution)/shard_map/ppermute | solution.py:248
  33.4 8.4 %collective-permute-start.6 = (bf16[6,128,256]{2,1,0:T(8,128)(2,1)S(1)}, bf16[6,128,256]{2,1,0:T(8,128)(2,1)S(1)}, u32[]{:S(2)}, u32[]{:S(2)}) collective-permute-start(bf16[6,128,256]{2,1,0:T(8,128)(2,1)S(1)} %collective-permute-done.2.refs_6_), channel_id=1, source_target_pairs={{0,8},{2,6},{8,16},{10,2},{16,24},{18,10},{24,28},{26,18},{28,20},... | collective-permute-start | bytes 1179656 | tf_op jit(solution)/shard_map/ppermute | solution.py:248
  35.2 10.8 %collective-permute-start.12 = (bf16[6,128,256]{2,1,0:T(8,128)(2,1)S(1)}, bf16[6,128,256]{2,1,0:T(8,128)(2,1)S(1)}, u32[]{:S(2)}, u32[]{:S(2)}) collective-permute-start(bf16[6,128,256]{2,1,0:T(8,128)(2,1)S(1)} %collective-permute-done.5.refs_7_), channel_id=1, source_target_pairs={{0,8},{2,6},{8,16},{10,2},{16,24},{18,10},{24,28},{26,18},{28,20},... | collective-permute-start | bytes 1179656 | tf_op jit(solution)/shard_map/ppermute | solution.py:248
  37.7 17.6 %collective-permute-start.18 = (bf16[15,2,128,256]{3,2,1,0:T(8,128)(2,1)S(1)}, bf16[15,2,128,256]{3,2,1,0:T(8,128)(2,1)S(1)}, u32[]{:S(2)}, u32[]{:S(2)}) collective-permute-start(bf16[15,2,128,256]{3,2,1,0:T(8,128)(2,1)S(1)} %sent.3), channel_id=1, source_target_pairs={{0,2},{2,0},{1,3},{3,1},{4,6},{6,4},{5,7},{7,5},{8,10},{10,8},{9,1... | collective-permute-start | bytes 5898248 | tf_op jit(solution)/shard_map/ppermute | solution.py:251
  37.8 14.9 %collective-permute-start.14 = (bf16[6,128,256]{2,1,0:T(8,128)(2,1)S(1)}, bf16[6,128,256]{2,1,0:T(8,128)(2,1)S(1)}, u32[]{:S(2)}, u32[]{:S(2)}) collective-permute-start(bf16[6,128,256]{2,1,0:T(8,128)(2,1)S(1)} %collective-permute-done.13.refs_2_), channel_id=1, source_target_pairs={{1,0},{0,1},{3,2},{2,3},{5,4},{4,5},{7,6},{6,7},{9,8},{8,9},{11,10... | collective-permute-start | bytes 1179656 | tf_op jit(solution)/shard_map/ppermute | solution.py:255
  41.8 11.0 %collective-permute-start.15 = (bf16[6,128,256]{2,1,0:T(8,128)(2,1)S(1)}, bf16[6,128,256]{2,1,0:T(8,128)(2,1)S(1)}, u32[]{:S(2)}, u32[]{:S(2)}) collective-permute-start(bf16[6,128,256]{2,1,0:T(8,128)(2,1)S(1)} %collective-permute-done.6.refs_0_), channel_id=1, source_target_pairs={{0,8},{2,6},{8,16},{10,2},{16,24},{18,10},{24,28},{26,18},{28,20},... | collective-permute-start | bytes 1179656 | tf_op jit(solution)/shard_map/ppermute | solution.py:248
  46.0 8.4 %collective-permute-start.16 = (bf16[6,128,256]{2,1,0:T(8,128)(2,1)S(1)}, bf16[6,128,256]{2,1,0:T(8,128)(2,1)S(1)}, u32[]{:S(2)}, u32[]{:S(2)}) collective-permute-start(bf16[6,128,256]{2,1,0:T(8,128)(2,1)S(1)} %collective-permute-done.12.refs_1_), channel_id=1, source_target_pairs={{0,8},{2,6},{8,16},{10,2},{16,24},{18,10},{24,28},{26,18},{28,20},... | collective-permute-start | bytes 1179656 | tf_op jit(solution)/shard_map/ppermute | solution.py:248
  55.3 2.9 %collective-permute-start.17 = (bf16[9,2,128,256]{3,2,1,0:T(8,128)(2,1)S(1)}, bf16[9,2,128,256]{3,2,1,0:T(8,128)(2,1)S(1)}, u32[]{:S(2)}, u32[]{:S(2)}) collective-permute-start(bf16[9,2,128,256]{3,2,1,0:T(8,128)(2,1)S(1)} %sent.2), channel_id=1, source_target_pairs={{0,2},{2,0},{1,3},{3,1},{4,6},{6,4},{5,7},{7,5},{8,10},{10,8},{9,1... | collective-permute-start | bytes 3538952 | tf_op jit(solution)/shard_map/ppermute | solution.py:251
  62.5 4.4 %copy-start = (f32[4,128,256]{2,1,0:T(8,128)}, f32[4,128,256]{2,1,0:T(8,128)S(1)}, u32[]{:S(2)}) copy-start(f32[4,128,256]{2,1,0:T(8,128)S(1)} %get-tuple-element.33) | copy-start | bytes 1572868
  62.5 9.3 %collective-permute-start.19 = (bf16[4,128,256]{2,1,0:T(8,128)(2,1)S(1)}, bf16[4,128,256]{2,1,0:T(8,128)(2,1)}, u32[]{:S(2)}, u32[]{:S(2)}) collective-permute-start(bf16[4,128,256]{2,1,0:T(8,128)(2,1)S(1)} %bitcast.2), channel_id=1, source_target_pairs={{0,1},{1,0},{2,3},{3,2},{4,5},{5,4},{6,7},{7,6},{8,9},{9,8},{10,11... | collective-permute-start | bytes 786440 | tf_op jit(solution)/shard_map/ppermute | solution.py:380
  66.9 6.9 %collective-permute-start.20 = (bf16[2,128,256]{2,1,0:T(8,128)(2,1)S(1)}, bf16[2,128,256]{2,1,0:T(8,128)(2,1)S(1)}, u32[]{:S(2)}, u32[]{:S(2)}) collective-permute-start(bf16[2,128,256]{2,1,0:T(8,128)(2,1)S(1)} %bitcast.3), channel_id=1, source_target_pairs={{0,1},{1,0},{2,3},{3,2},{4,5},{5,4},{6,7},{7,6},{8,9},{9,8},{10,11... | collective-permute-start | bytes 393224 | tf_op jit(solution)/shard_map/ppermute | solution.py:380
  (2 other events, 1.3 us)

commit v3 on v2

--- a/solution.py
+++ b/solution.py
@@ -288,7 +288,7 @@
         [scalars] * 3 + [apart],
     )
 
-    rules = {'other': [('crossed', -2)], ('crossed', 2): [('beside', -1)], ('own', 3): [('beside', -1)]}
+    rules = {'other': [('crossed', -2)], ('other', 2): [('own', -1)]}
 
     @functools.cache
     def arrived(kind, k):
@@ -335,12 +335,12 @@
         )
         return swap(sent)
 
-    first_received = gather(0, early, flat(0, early, (('crossed', 2),)))
+    first_received = gather(0, early, flat(0, early, ()))
     operators_out = [jax.ShapeDtypeStruct(x.shape, jnp.bfloat16) for x in (left_ops, right_ops)]
     lefts, rights, blocks = call(
         functools.partial(load_kernel, sizes, early),
         "load",
-        [table, left_ops, right_ops] + flat(0, early, ()),
+        [table, left_ops, right_ops] + flat(0, early, (('own', 3),)),
         operators_out + [blocks_out],
         [pltpu.SemaphoreType.DMA((asked,)), pltpu.SemaphoreType.DMA((3,))],
         [whole] + [apart] * 2 + [held_in] * (early * op_size),

time: 74.9 us -> 74.9 us (level)
    ppermute x4, waiting for transfers between devices: 0.46 us -> 2.24 us  [across(): lax.ppermute(x, 'op', [((q + j) % op_size, q) for q in range(op_size)])]
    ppermute x11, waiting for transfers between devices: 15.3 us -> 13.9 us  [hop(): return lax.ppermute(x, ('chip', 'core'), pairs)]
  transfers between devices with their start and end apart: 21 -> 21, of which waited for: 11 -> 13; matrix products, arithmetic and copies ran while one was open for 2% -> 2% of each run, Pallas kernels for 18% -> 18%
where the time goes in v3:
time: 74.9 us; the launch traced here: 74.6 us
  starting transfers between devices  28.7 us (38%)
  waiting for transfers between devices  23.1 us (31%)
  Pallas kernels  17.6 us (23%)
  local copies, waits for them, and re-layouts  3.03 us (4%)
  other arithmetic  1.98 us (3%)
    ppermute x11, starting transfers between devices, hop(): return lax.ppermute(x, ('chip', 'core'), pairs)  18.9 us
    pallas_call x7, Pallas kernels, call(): pl.pallas_call(kernel, name=name, in_specs=specs or [whole] + [held_in] *...  17.6 us
    ppermute x11, waiting for transfers between devices, hop(): return lax.ppermute(x, ('chip', 'core'), pairs)  13.9 us
    ppermute x4, starting transfers between devices, across(): lax.ppermute(x, 'op', [((q + j) % op_size, q) for q in range(op_size)])  7.1 us
    ppermute x2, waiting for transfers between devices, shards(): part = lax.ppermute(send[k - 1], 'op', turn)  5.34 us
    unnamed x10, local copies, waits for them, and re-layouts  3.03 us
    ppermute x4, waiting for transfers between devices, across(): lax.ppermute(x, 'op', [((q + j) % op_size, q) for q in range(op_size)])  2.24 us
    ppermute x2, starting transfers between devices, shards(): part = lax.ppermute(send[k - 1], 'op', turn)  2.17 us
  transfers between devices with their start and end apart: 21, of which 13 were waited for; matrix products, arithmetic and copies ran while one was open for 2% of the time, Pallas kernels for 18%

profile of v3, /device:TPU:0, one launch (start us, length us, event | category | flops | bytes accessed | tf_op | source)
XLA Modules:
  0.0 74.6 jit_solution(330421102097438061)
XLA Ops:
  0.5 2.5 %collective-permute-start.4 = (bf16[6,128,256]{2,1,0:T(8,128)(2,1)}, bf16[6,128,256]{2,1,0:T(8,128)(2,1)S(1)}, u32[]{:S(2)}, u32[]{:S(2)}) collective-permute-start(bf16[6,128,256]{2,1,0:T(8,128)(2,1)} %wave.1), channel_id=1, source_target_pairs={{1,0},{0,1},{3,2},{2,3},{5,4},{4,5},{7,6},{6,7},{9,8},{8,9},{11,10... | collective-permute-start | bytes 1179656 | tf_op jit(solution)/shard_map/ppermute | solution.py:255
  2.9 1.6 %collective-permute-start.1 = (bf16[6,128,256]{2,1,0:T(8,128)(2,1)}, bf16[6,128,256]{2,1,0:T(8,128)(2,1)S(1)}, u32[]{:S(2)}, u32[]{:S(2)}) collective-permute-start(bf16[6,128,256]{2,1,0:T(8,128)(2,1)} %wave.1), channel_id=1, source_target_pairs={{0,8},{2,6},{8,16},{10,2},{16,24},{18,10},{24,28},{26,18},{28,20},... | collective-permute-start | bytes 1179656 | tf_op jit(solution)/shard_map/ppermute | solution.py:248
  4.5 1.6 %collective-permute-start.7 = (bf16[6,128,256]{2,1,0:T(8,128)(2,1)S(1)}, bf16[6,128,256]{2,1,0:T(8,128)(2,1)S(1)}, u32[]{:S(2)}, u32[]{:S(2)}) collective-permute-start(bf16[6,128,256]{2,1,0:T(8,128)(2,1)S(1)} %collective-permute-done.6), channel_id=1, source_target_pairs={{0,8},{2,6},{8,16},{10,2},{16,24},{18,10},{24,28},{26,18},{28,20},... | collective-permute-start | bytes 1179656 | tf_op jit(solution)/shard_map/ppermute | solution.py:248
  9.1 2.9 %table.1 = (s32[8,128]{1,0:T(8,128)S(1)}, bf16[6,128,256]{2,1,0:T(8,128)(2,1)S(1)}) custom-call(s32[6,5]{1,0:T(8,128)S(1)} %copy-done.2, s32[6,5]{1,0:T(8,128)S(1)} %copy-done.3, s32[8]{0:T(128)S(1)} %copy-done.4, bf16[6,128,256]{2,1,0:T(8,128)(2,1)S(1)} %copy-done.1), custom_call_target="tpu_custom_call" | custom-call | bytes 395264 | tf_op jit(solution)/shard_map/table/pallas_call | solution.py:264
  12.9 1.8 %collective-permute-start.5 = (bf16[6,128,256]{2,1,0:T(8,128)(2,1)S(1)}, bf16[6,128,256]{2,1,0:T(8,128)(2,1)S(1)}, u32[]{:S(2)}, u32[]{:S(2)}) collective-permute-start(bf16[6,128,256]{2,1,0:T(8,128)(2,1)S(1)} %collective-permute-done.4.refs_1_), channel_id=1, source_target_pairs={{0,8},{2,6},{8,16},{10,2},{16,24},{18,10},{24,28},{26,18},{28,20},... | collective-permute-start | bytes 1179656 | tf_op jit(solution)/shard_map/ppermute | solution.py:248
  20.7 1.8 %collective-permute-start.9 = (bf16[6,128,256]{2,1,0:T(8,128)(2,1)S(1)}, bf16[6,128,256]{2,1,0:T(8,128)(2,1)S(1)}, u32[]{:S(2)}, u32[]{:S(2)}) collective-permute-start(bf16[6,128,256]{2,1,0:T(8,128)(2,1)S(1)} %collective-permute-done.5.refs_3_), channel_id=1, source_target_pairs={{0,8},{2,6},{8,16},{10,2},{16,24},{18,10},{24,28},{26,18},{28,20},... | collective-permute-start | bytes 1179656 | tf_op jit(solution)/shard_map/ppermute | solution.py:248
  22.5 2.4 %collective-permute-done.10.refs_8_ = bf16[6,128,256]{2,1,0:T(8,128)(2,1)S(1)} collective-permute-done((bf16[6,128,256]{2,1,0:T(8,128)(2,1)S(1)}, bf16[6,128,256]{2,1,0:T(8,128)(2,1)S(1)}, u32[]{:S(2)}, u32[]{:S(2)}) %collective-permute-start.10) | collective-permute-done | bytes 393248 | tf_op jit(solution)/shard_map/ppermute | solution.py:248
  24.9 1.7 %collective-permute-start.11 = (bf16[6,128,256]{2,1,0:T(8,128)(2,1)S(1)}, bf16[6,128,256]{2,1,0:T(8,128)(2,1)S(1)}, u32[]{:S(2)}, u32[]{:S(2)}) collective-permute-start(bf16[6,128,256]{2,1,0:T(8,128)(2,1)S(1)} %collective-permute-done.10.refs_8_), channel_id=1, source_target_pairs={{1,0},{0,1},{3,2},{2,3},{5,4},{4,5},{7,6},{6,7},{9,8},{8,9},{11,10... | collective-permute-start | bytes 1179656 | tf_op jit(solution)/shard_map/ppermute | solution.py:255
  26.7 2.5 %collective-permute-done.2.refs_6_ = bf16[6,128,256]{2,1,0:T(8,128)(2,1)S(1)} collective-permute-done((bf16[6,128,256]{2,1,0:T(8,128)(2,1)S(1)}, bf16[6,128,256]{2,1,0:T(8,128)(2,1)S(1)}, u32[]{:S(2)}, u32[]{:S(2)}) %collective-permute-start.2) | collective-permute-done | bytes 393248 | tf_op jit(solution)/shard_map/ppermute | solution.py:248
  29.1 1.8 %collective-permute-start.3 = (bf16[6,128,256]{2,1,0:T(8,128)(2,1)S(1)}, bf16[6,128,256]{2,1,0:T(8,128)(2,1)S(1)}, u32[]{:S(2)}, u32[]{:S(2)}) collective-permute-start(bf16[6,128,256]{2,1,0:T(8,128)(2,1)S(1)} %collective-permute-done.2.refs_6_), channel_id=1, source_target_pairs={{0,8},{2,6},{8,16},{10,2},{16,24},{18,10},{24,28},{26,18},{28,20},... | collective-permute-start | bytes 1179656 | tf_op jit(solution)/shard_map/ppermute | solution.py:248
  31.0 1.6 %collective-permute-start.13 = (bf16[6,128,256]{2,1,0:T(8,128)(2,1)S(1)}, bf16[6,128,256]{2,1,0:T(8,128)(2,1)S(1)}, u32[]{:S(2)}, u32[]{:S(2)}) collective-permute-start(bf16[6,128,256]{2,1,0:T(8,128)(2,1)S(1)} %collective-permute-done.10.refs_8_), channel_id=1, source_target_pairs={{0,8},{2,6},{8,16},{10,2},{16,24},{18,10},{24,28},{26,18},{28,20},... | collective-permute-start | bytes 1179656 | tf_op jit(solution)/shard_map/ppermute | solution.py:248
  33.4 1.8 %collective-permute-start.12 = (bf16[6,128,256]{2,1,0:T(8,128)(2,1)S(1)}, bf16[6,128,256]{2,1,0:T(8,128)(2,1)S(1)}, u32[]{:S(2)}, u32[]{:S(2)}) collective-permute-start(bf16[6,128,256]{2,1,0:T(8,128)(2,1)S(1)} %collective-permute-done.9.refs_7_), channel_id=1, source_target_pairs={{0,8},{2,6},{8,16},{10,2},{16,24},{18,10},{24,28},{26,18},{28,20},... | collective-permute-start | bytes 1179656 | tf_op jit(solution)/shard_map/ppermute | solution.py:248
  37.6 1.8 %collective-permute-start.15 = (bf16[6,128,256]{2,1,0:T(8,128)(2,1)S(1)}, bf16[6,128,256]{2,1,0:T(8,128)(2,1)S(1)}, u32[]{:S(2)}, u32[]{:S(2)}) collective-permute-start(bf16[6,128,256]{2,1,0:T(8,128)(2,1)S(1)} %collective-permute-done.3.refs_0_), channel_id=1, source_target_pairs={{0,8},{2,6},{8,16},{10,2},{16,24},{18,10},{24,28},{26,18},{28,20},... | collective-permute-start | bytes 1179656 | tf_op jit(solution)/shard_map/ppermute | solution.py:248
  39.4 2.4 %collective-permute-done.13.refs_2_ = bf16[6,128,256]{2,1,0:T(8,128)(2,1)S(1)} collective-permute-done((bf16[6,128,256]{2,1,0:T(8,128)(2,1)S(1)}, bf16[6,128,256]{2,1,0:T(8,128)(2,1)S(1)}, u32[]{:S(2)}, u32[]{:S(2)}) %collective-permute-start.13) | collective-permute-done | bytes 393248 | tf_op jit(solution)/shard_map/ppermute | solution.py:248
  41.8 1.7 %collective-permute-start.14 = (bf16[6,128,256]{2,1,0:T(8,128)(2,1)S(1)}, bf16[6,128,256]{2,1,0:T(8,128)(2,1)S(1)}, u32[]{:S(2)}, u32[]{:S(2)}) collective-permute-start(bf16[6,128,256]{2,1,0:T(8,128)(2,1)S(1)} %collective-permute-done.13.refs_2_), channel_id=1, source_target_pairs={{1,0},{0,1},{3,2},{2,3},{5,4},{4,5},{7,6},{6,7},{9,8},{8,9},{11,10... | collective-permute-start | bytes 1179656 | tf_op jit(solution)/shard_map/ppermute | solution.py:255
  43.5 2.5 %collective-permute-done.12.refs_1_ = bf16[6,128,256]{2,1,0:T(8,128)(2,1)S(1)} collective-permute-done((bf16[6,128,256]{2,1,0:T(8,128)(2,1)S(1)}, bf16[6,128,256]{2,1,0:T(8,128)(2,1)S(1)}, u32[]{:S(2)}, u32[]{:S(2)}) %collective-permute-start.12) | collective-permute-done | bytes 393248 | tf_op jit(solution)/shard_map/ppermute | solution.py:248
  46.0 1.8 %collective-permute-start.16 = (bf16[6,128,256]{2,1,0:T(8,128)(2,1)S(1)}, bf16[6,128,256]{2,1,0:T(8,128)(2,1)S(1)}, u32[]{:S(2)}, u32[]{:S(2)}) collective-permute-start(bf16[6,128,256]{2,1,0:T(8,128)(2,1)S(1)} %collective-permute-done.12.refs_1_), channel_id=1, source_target_pairs={{0,8},{2,6},{8,16},{10,2},{16,24},{18,10},{24,28},{26,18},{28,20},... | collective-permute-start | bytes 1179656 | tf_op jit(solution)/shard_map/ppermute | solution.py:248
  47.8 4.9 %load.1 = (bf16[6,8,256,256]{3,2,1,0:T(8,128)(2,1)S(1)}, bf16[6,8,256,256]{3,2,1,0:T(8,128)(2,1)S(1)}, bf16[30,2,128,256]{3,2,1,0:T(8,128)(2,1)S(1)}) custom-call(s32[8,128]{1,0:T(8,128)S(1)} %get-tuple-element.21.table_in, bf16[6,8,256,256]{3,2,1,0:T(8,128)(2,1)} %left.1, bf16[6,8,256,256]{3,2,1,0:T(8,128)(2,1)} %right.1, ...), custom_call_target="tpu_custom_call" | custom-call | bytes 16515072 | tf_op jit(solution)/shard_map/load/pallas_call | solution.py:264
  52.8 1.7 %collective-permute-done.16.refs_5_ = bf16[6,128,256]{2,1,0:T(8,128)(2,1)S(1)} collective-permute-done((bf16[6,128,256]{2,1,0:T(8,128)(2,1)S(1)}, bf16[6,128,256]{2,1,0:T(8,128)(2,1)S(1)}, u32[]{:S(2)}, u32[]{:S(2)}) %collective-permute-start.16) | collective-permute-done | bytes 393248 | tf_op jit(solution)/shard_map/ppermute | solution.py:248
  56.5 1.7 %collective-permute-done.17.received = bf16[9,2,128,256]{3,2,1,0:T(8,128)(2,1)S(1)} collective-permute-done((bf16[9,2,128,256]{3,2,1,0:T(8,128)(2,1)S(1)}, bf16[9,2,128,256]{3,2,1,0:T(8,128)(2,1)S(1)}, u32[]{:S(2)}, u32[]{:S(2)}) %collective-permute-start.17) | collective-permute-done | bytes 1179680 | tf_op jit(solution)/shard_map/ppermute | solution.py:251
  58.2 4.3 %product.2 = (f32[4,128,256]{2,1,0:T(8,128)S(1)}, bf16[1,4,128,256]{3,2,1,0:T(8,128)(2,1)S(1)}, bf16[30,2,128,256]{3,2,1,0:T(8,128)(2,1)S(1)}) custom-call(s32[8,128]{1,0:T(8,128)S(1)} %get-tuple-element.21.table_in, bf16[9,2,128,256]{3,2,1,0:T(8,128)(2,1)S(1)} %collective-permute-done.17.received, ...), custom_call_target="tpu_custom_call", output_to_operand_aliasing={{2}: (4, {})} | custom-call | flops 2147483648 | bytes 4456448 | tf_op jit(solution)/shard_map/product/pallas_call | solution.py:264
  62.6 1.8 %collective-permute-start.19 = (bf16[4,128,256]{2,1,0:T(8,128)(2,1)S(1)}, bf16[4,128,256]{2,1,0:T(8,128)(2,1)}, u32[]{:S(2)}, u32[]{:S(2)}) collective-permute-start(bf16[4,128,256]{2,1,0:T(8,128)(2,1)S(1)} %bitcast.2), channel_id=1, source_target_pairs={{0,1},{1,0},{2,3},{3,2},{4,5},{5,4},{6,7},{7,6},{8,9},{9,8},{10,11... | collective-permute-start | bytes 786440 | tf_op jit(solution)/shard_map/ppermute | solution.py:380
  64.4 2.6 %product.3 = (f32[2,128,256]{2,1,0:T(8,128)S(1)}, bf16[1,2,128,256]{3,2,1,0:T(8,128)(2,1)S(1)}, bf16[30,2,128,256]{3,2,1,0:T(8,128)(2,1)S(1)}) custom-call(s32[8,128]{1,0:T(8,128)S(1)} %get-tuple-element.21.table_in, bf16[9,2,128,256]{3,2,1,0:T(8,128)(2,1)S(1)} %collective-permute-done.17.received, ...), custom_call_target="tpu_custom_call", output_to_operand_aliasing={{2}: (4, {})} | custom-call | flops 1073741824 | bytes 4194304 | tf_op jit(solution)/shard_map/product/pallas_call | solution.py:264
  67.3 4.6 %collective-permute-done.19.source = bf16[4,128,256]{2,1,0:T(8,128)(2,1)} collective-permute-done((bf16[4,128,256]{2,1,0:T(8,128)(2,1)S(1)}, bf16[4,128,256]{2,1,0:T(8,128)(2,1)}, u32[]{:S(2)}, u32[]{:S(2)}) %collective-permute-start.19) | collective-permute-done | bytes 262176 | tf_op jit(solution)/shard_map/ppermute | solution.py:380
  (39 shorter events, 18.7 us)
Async XLA Ops:
  0.0 4.5 %collective-permute-start.6 = (bf16[6,128,256]{2,1,0:T(8,128)(2,1)}, bf16[6,128,256]{2,1,0:T(8,128)(2,1)S(1)}, u32[]{:S(2)}, u32[]{:S(2)}) collective-permute-start(bf16[6,128,256]{2,1,0:T(8,128)(2,1)} %wave.1), channel_id=1, source_target_pairs={{0,2},{2,0},{1,3},{3,1},{4,6},{6,4},{5,7},{7,5},{8,10},{10,8},{9,1... | collective-permute-start | bytes 1179656 | tf_op jit(solution)/shard_map/ppermute | solution.py:251
  0.5 12.5 %collective-permute-start.4 = (bf16[6,128,256]{2,1,0:T(8,128)(2,1)}, bf16[6,128,256]{2,1,0:T(8,128)(2,1)S(1)}, u32[]{:S(2)}, u32[]{:S(2)}) collective-permute-start(bf16[6,128,256]{2,1,0:T(8,128)(2,1)} %wave.1), channel_id=1, source_target_pairs={{1,0},{0,1},{3,2},{2,3},{5,4},{4,5},{7,6},{6,7},{9,8},{8,9},{11,10... | collective-permute-start | bytes 1179656 | tf_op jit(solution)/shard_map/ppermute | solution.py:255
  2.9 11.8 %collective-permute-start.1 = (bf16[6,128,256]{2,1,0:T(8,128)(2,1)}, bf16[6,128,256]{2,1,0:T(8,128)(2,1)S(1)}, u32[]{:S(2)}, u32[]{:S(2)}) collective-permute-start(bf16[6,128,256]{2,1,0:T(8,128)(2,1)} %wave.1), channel_id=1, source_target_pairs={{0,8},{2,6},{8,16},{10,2},{16,24},{18,10},{24,28},{26,18},{28,20},... | collective-permute-start | bytes 1179656 | tf_op jit(solution)/shard_map/ppermute | solution.py:248
  4.5 10.6 %collective-permute-start.7 = (bf16[6,128,256]{2,1,0:T(8,128)(2,1)S(1)}, bf16[6,128,256]{2,1,0:T(8,128)(2,1)S(1)}, u32[]{:S(2)}, u32[]{:S(2)}) collective-permute-start(bf16[6,128,256]{2,1,0:T(8,128)(2,1)S(1)} %collective-permute-done.6), channel_id=1, source_target_pairs={{0,8},{2,6},{8,16},{10,2},{16,24},{18,10},{24,28},{26,18},{28,20},... | collective-permute-start | bytes 1179656 | tf_op jit(solution)/shard_map/ppermute | solution.py:248
  6.1 1.0 %copy-start.1 = (bf16[6,128,256]{2,1,0:T(8,128)(2,1)S(1)}, bf16[6,128,256]{2,1,0:T(8,128)(2,1)}, u32[]{:S(2)}) copy-start(bf16[6,128,256]{2,1,0:T(8,128)(2,1)} %wave.1) | copy-start | bytes 1179652
  7.1 0.7 copy-start.2
  12.9 7.8 %collective-permute-start.5 = (bf16[6,128,256]{2,1,0:T(8,128)(2,1)S(1)}, bf16[6,128,256]{2,1,0:T(8,128)(2,1)S(1)}, u32[]{:S(2)}, u32[]{:S(2)}) collective-permute-start(bf16[6,128,256]{2,1,0:T(8,128)(2,1)S(1)} %collective-permute-done.4.refs_1_), channel_id=1, source_target_pairs={{0,8},{2,6},{8,16},{10,2},{16,24},{18,10},{24,28},{26,18},{28,20},... | collective-permute-start | bytes 1179656 | tf_op jit(solution)/shard_map/ppermute | solution.py:248
  15.1 9.8 %collective-permute-start.10 = (bf16[6,128,256]{2,1,0:T(8,128)(2,1)S(1)}, bf16[6,128,256]{2,1,0:T(8,128)(2,1)S(1)}, u32[]{:S(2)}, u32[]{:S(2)}) collective-permute-start(bf16[6,128,256]{2,1,0:T(8,128)(2,1)S(1)} %collective-permute-done.7.refs_4_), channel_id=1, source_target_pairs={{0,8},{2,6},{8,16},{10,2},{16,24},{18,10},{24,28},{26,18},{28,20},... | collective-permute-start | bytes 1179656 | tf_op jit(solution)/shard_map/ppermute | solution.py:248
  16.7 12.4 %collective-permute-start.2 = (bf16[6,128,256]{2,1,0:T(8,128)(2,1)S(1)}, bf16[6,128,256]{2,1,0:T(8,128)(2,1)S(1)}, u32[]{:S(2)}, u32[]{:S(2)}) collective-permute-start(bf16[6,128,256]{2,1,0:T(8,128)(2,1)S(1)} %collective-permute-done.1.refs_2_), channel_id=1, source_target_pairs={{0,8},{2,6},{8,16},{10,2},{16,24},{18,10},{24,28},{26,18},{28,20},... | collective-permute-start | bytes 1179656 | tf_op jit(solution)/shard_map/ppermute | solution.py:248
  18.3 12.7 %collective-permute-start.8 = (bf16[6,128,256]{2,1,0:T(8,128)(2,1)S(1)}, bf16[6,128,256]{2,1,0:T(8,128)(2,1)S(1)}, u32[]{:S(2)}, u32[]{:S(2)}) collective-permute-start(bf16[6,128,256]{2,1,0:T(8,128)(2,1)S(1)} %collective-permute-done.7.refs_4_), channel_id=1, source_target_pairs={{1,0},{0,1},{3,2},{2,3},{5,4},{4,5},{7,6},{6,7},{9,8},{8,9},{11,10... | collective-permute-start | bytes 1179656 | tf_op jit(solution)/shard_map/ppermute | solution.py:255
  20.7 12.6 %collective-permute-start.9 = (bf16[6,128,256]{2,1,0:T(8,128)(2,1)S(1)}, bf16[6,128,256]{2,1,0:T(8,128)(2,1)S(1)}, u32[]{:S(2)}, u32[]{:S(2)}) collective-permute-start(bf16[6,128,256]{2,1,0:T(8,128)(2,1)S(1)} %collective-permute-done.5.refs_3_), channel_id=1, source_target_pairs={{0,8},{2,6},{8,16},{10,2},{16,24},{18,10},{24,28},{26,18},{28,20},... | collective-permute-start | bytes 1179656 | tf_op jit(solution)/shard_map/ppermute | solution.py:248
  24.9 11.6 %collective-permute-start.11 = (bf16[6,128,256]{2,1,0:T(8,128)(2,1)S(1)}, bf16[6,128,256]{2,1,0:T(8,128)(2,1)S(1)}, u32[]{:S(2)}, u32[]{:S(2)}) collective-permute-start(bf16[6,128,256]{2,1,0:T(8,128)(2,1)S(1)} %collective-permute-done.10.refs_8_), channel_id=1, source_target_pairs={{1,0},{0,1},{3,2},{2,3},{5,4},{4,5},{7,6},{6,7},{9,8},{8,9},{11,10... | collective-permute-start | bytes 1179656 | tf_op jit(solution)/shard_map/ppermute | solution.py:255
  26.7 8.5 %collective-permute-start = (s32[8,128]{1,0:T(8,128)S(1)}, s32[8,128]{1,0:T(8,128)S(1)}, u32[]{:S(2)}, u32[]{:S(2)}) collective-permute-start(s32[8,128]{1,0:T(8,128)S(1)} %get-tuple-element.21.table_in), channel_id=1, source_target_pairs={{0,2},{2,0},{1,3},{3,1},{4,6},{6,4},{5,7},{7,5},{8,10},{10,8},{9,1... | collective-permute-start | bytes 12296 | tf_op jit(solution)/shard_map/ppermute | solution.py:251
  29.1 8.4 %collective-permute-start.3 = (bf16[6,128,256]{2,1,0:T(8,128)(2,1)S(1)}, bf16[6,128,256]{2,1,0:T(8,128)(2,1)S(1)}, u32[]{:S(2)}, u32[]{:S(2)}) collective-permute-start(bf16[6,128,256]{2,1,0:T(8,128)(2,1)S(1)} %collective-permute-done.2.refs_6_), channel_id=1, source_target_pairs={{0,8},{2,6},{8,16},{10,2},{16,24},{18,10},{24,28},{26,18},{28,20},... | collective-permute-start | bytes 1179656 | tf_op jit(solution)/shard_map/ppermute | solution.py:248
  31.0 10.8 %collective-permute-start.13 = (bf16[6,128,256]{2,1,0:T(8,128)(2,1)S(1)}, bf16[6,128,256]{2,1,0:T(8,128)(2,1)S(1)}, u32[]{:S(2)}, u32[]{:S(2)}) collective-permute-start(bf16[6,128,256]{2,1,0:T(8,128)(2,1)S(1)} %collective-permute-done.10.refs_8_), channel_id=1, source_target_pairs={{0,8},{2,6},{8,16},{10,2},{16,24},{18,10},{24,28},{26,18},{28,20},... | collective-permute-start | bytes 1179656 | tf_op jit(solution)/shard_map/ppermute | solution.py:248
  33.4 12.6 %collective-permute-start.12 = (bf16[6,128,256]{2,1,0:T(8,128)(2,1)S(1)}, bf16[6,128,256]{2,1,0:T(8,128)(2,1)S(1)}, u32[]{:S(2)}, u32[]{:S(2)}) collective-permute-start(bf16[6,128,256]{2,1,0:T(8,128)(2,1)S(1)} %collective-permute-done.9.refs_7_), channel_id=1, source_target_pairs={{0,8},{2,6},{8,16},{10,2},{16,24},{18,10},{24,28},{26,18},{28,20},... | collective-permute-start | bytes 1179656 | tf_op jit(solution)/shard_map/ppermute | solution.py:248
  37.5 17.9 %collective-permute-start.18 = (bf16[15,2,128,256]{3,2,1,0:T(8,128)(2,1)S(1)}, bf16[15,2,128,256]{3,2,1,0:T(8,128)(2,1)S(1)}, u32[]{:S(2)}, u32[]{:S(2)}) collective-permute-start(bf16[15,2,128,256]{3,2,1,0:T(8,128)(2,1)S(1)} %sent.3), channel_id=1, source_target_pairs={{0,2},{2,0},{1,3},{3,1},{4,6},{6,4},{5,7},{7,5},{8,10},{10,8},{9,1... | collective-permute-start | bytes 5898248 | tf_op jit(solution)/shard_map/ppermute | solution.py:251
  37.6 15.2 %collective-permute-start.15 = (bf16[6,128,256]{2,1,0:T(8,128)(2,1)S(1)}, bf16[6,128,256]{2,1,0:T(8,128)(2,1)S(1)}, u32[]{:S(2)}, u32[]{:S(2)}) collective-permute-start(bf16[6,128,256]{2,1,0:T(8,128)(2,1)S(1)} %collective-permute-done.3.refs_0_), channel_id=1, source_target_pairs={{0,8},{2,6},{8,16},{10,2},{16,24},{18,10},{24,28},{26,18},{28,20},... | collective-permute-start | bytes 1179656 | tf_op jit(solution)/shard_map/ppermute | solution.py:248
  41.8 11.0 %collective-permute-start.14 = (bf16[6,128,256]{2,1,0:T(8,128)(2,1)S(1)}, bf16[6,128,256]{2,1,0:T(8,128)(2,1)S(1)}, u32[]{:S(2)}, u32[]{:S(2)}) collective-permute-start(bf16[6,128,256]{2,1,0:T(8,128)(2,1)S(1)} %collective-permute-done.13.refs_2_), channel_id=1, source_target_pairs={{1,0},{0,1},{3,2},{2,3},{5,4},{4,5},{7,6},{6,7},{9,8},{8,9},{11,10... | collective-permute-start | bytes 1179656 | tf_op jit(solution)/shard_map/ppermute | solution.py:255
  46.0 8.4 %collective-permute-start.16 = (bf16[6,128,256]{2,1,0:T(8,128)(2,1)S(1)}, bf16[6,128,256]{2,1,0:T(8,128)(2,1)S(1)}, u32[]{:S(2)}, u32[]{:S(2)}) collective-permute-start(bf16[6,128,256]{2,1,0:T(8,128)(2,1)S(1)} %collective-permute-done.12.refs_1_), channel_id=1, source_target_pairs={{0,8},{2,6},{8,16},{10,2},{16,24},{18,10},{24,28},{26,18},{28,20},... | collective-permute-start | bytes 1179656 | tf_op jit(solution)/shard_map/ppermute | solution.py:248
  55.3 2.9 %collective-permute-start.17 = (bf16[9,2,128,256]{3,2,1,0:T(8,128)(2,1)S(1)}, bf16[9,2,128,256]{3,2,1,0:T(8,128)(2,1)S(1)}, u32[]{:S(2)}, u32[]{:S(2)}) collective-permute-start(bf16[9,2,128,256]{3,2,1,0:T(8,128)(2,1)S(1)} %sent.2), channel_id=1, source_target_pairs={{0,2},{2,0},{1,3},{3,1},{4,6},{6,4},{5,7},{7,5},{8,10},{10,8},{9,1... | collective-permute-start | bytes 3538952 | tf_op jit(solution)/shard_map/ppermute | solution.py:251
  62.5 4.4 %copy-start = (f32[4,128,256]{2,1,0:T(8,128)}, f32[4,128,256]{2,1,0:T(8,128)S(1)}, u32[]{:S(2)}) copy-start(f32[4,128,256]{2,1,0:T(8,128)S(1)} %get-tuple-element.31) | copy-start | bytes 1572868
  62.6 9.3 %collective-permute-start.19 = (bf16[4,128,256]{2,1,0:T(8,128)(2,1)S(1)}, bf16[4,128,256]{2,1,0:T(8,128)(2,1)}, u32[]{:S(2)}, u32[]{:S(2)}) collective-permute-start(bf16[4,128,256]{2,1,0:T(8,128)(2,1)S(1)} %bitcast.2), channel_id=1, source_target_pairs={{0,1},{1,0},{2,3},{3,2},{4,5},{5,4},{6,7},{7,6},{8,9},{9,8},{10,11... | collective-permute-start | bytes 786440 | tf_op jit(solution)/shard_map/ppermute | solution.py:380
  67.0 6.8 %collective-permute-start.20 = (bf16[2,128,256]{2,1,0:T(8,128)(2,1)S(1)}, bf16[2,128,256]{2,1,0:T(8,128)(2,1)S(1)}, u32[]{:S(2)}, u32[]{:S(2)}) collective-permute-start(bf16[2,128,256]{2,1,0:T(8,128)(2,1)S(1)} %bitcast.3), channel_id=1, source_target_pairs={{0,1},{1,0},{2,3},{3,2},{4,5},{5,4},{6,7},{7,6},{8,9},{9,8},{10,11... | collective-permute-start | bytes 393224 | tf_op jit(solution)/shard_map/ppermute | solution.py:380
  (2 other events, 1.3 us)
